TPU v7x, 256 devices: a whole 4x4x8 slice. The times are simulated.
256 devices in a mesh: east: 8 (over z_hi, core), north: 32 (over y, z_lo, x).
Axes of the slice: x: 4, y: 4, z: 8 (z_hi: 4, z_lo: 2; z = z_hi * 2 + z_lo), core: 2. Of those that a mesh axis runs over, the one named last changes fastest.
Arguments:
- adjoint_start: float32 [5, 128, 1024, 256], P(None, 'east', 'north'), may hold values from -3 to 3
- adjoint_source: float32 [5, 128, 1024, 256], P(None, 'east', 'north'), may hold values from -6 to 6
- base_flow: float32 [3, 128, 1024, 256], P(None, 'east', 'north'), may hold values from -3 to 3
- eddy_visc: float32 [128, 1024, 256], P('east', 'north'), may hold values from 0.1 to 3
- rotor_count: int32 [8, 32], P('east', 'north'), may hold values from 128 to 1024, as said below
- rotor_cell: int32 [8, 32, 1024], P('east', 'north'), may hold values from 0 to 131071
- rotor_turbine: int32 [8, 32, 1024], P('east', 'north'), may hold values from 0 to 383
- rotor_sector: int32 [8, 32, 1024], P('east', 'north'), may hold values from 0 to 7
- rotor_weight: float32 [8, 32, 1024], P('east', 'north'), may hold values from 0.25 to 1
Outputs:
- adjoint_final: float32 [5, 128, 1024, 256], P(None, 'east', 'north')
- thrust_grad: float32 [4, 8, 384], P(None, None, 'north')
Inputs may be any that keep to these rules, and one draw needn't show every extreme that they name: `rotor_count`: an eighth of the tiles (at least one), drawn from the seed, hold 1024 live entries; the others hold 128 to 256.
All inputs are finite; a program needn't handle non-finite values.
Results may differ from a plain program's by a relative error of at most 0.0001.
Values sent between devices are 32-bit elements; how exact they have to be, the bound alone decides.
A program may use at most 192 MiB of HBM per device.

v0:
```python
import jax
import jax.numpy as jnp
from jax import lax
from jax.sharding import PartitionSpec as P

SECT = 8
TURB_DEV = 12


def extended(shard, sides, width):
    for axis, dim in sides:
        size, length = (lax.axis_size(axis), shard.shape[dim])
        up = [(i, (i + 1) % size) for i in range(size - 1)]
        down = [(j, i) for i, j in up]
        last = lax.slice_in_dim(shard, length - width, length, axis=dim)
        leading = lax.slice_in_dim(shard, 0, width, axis=dim)
        before = lax.ppermute(last, axis, up)
        after = lax.ppermute(leading, axis, down)
        shard = jnp.concatenate([before, shard, after], axis=dim)
    return shard


def spread(field):
    return jnp.pad(field, ((0, 0), (0, 0), (0, 0), (1, 1)))


def beside_all(padded):
    total = padded[:, 2:, 1:-1, 1:-1] + padded[:, :-2, 1:-1, 1:-1]
    total = total + padded[:, 1:-1, 2:, 1:-1] + padded[:, 1:-1, :-2, 1:-1]
    return total + padded[:, 1:-1, 1:-1, 2:] + padded[:, 1:-1, 1:-1, :-2]


def slopes(padded):
    return [
        padded[:, 2:, 1:-1, 1:-1] - padded[:, :-2, 1:-1, 1:-1],
        padded[:, 1:-1, 2:, 1:-1] - padded[:, 1:-1, :-2, 1:-1],
        padded[:, 1:-1, 1:-1, 2:] - padded[:, 1:-1, 1:-1, :-2],
    ]


def relax(state_pad, base_pad, source):
    full = spread(state_pad)
    base_full = spread(base_pad)
    centre = full[:, 1:-1, 1:-1, 1:-1]
    base_centre = base_full[:, 1:-1, 1:-1, 1:-1]
    neighbours = beside_all(full)
    diffs = slopes(full)
    velocity_base = base_centre[:3]
    viscous = 1.0 + base_centre[3]
    convect = (
        velocity_base[0] * diffs[0][:3]
        + velocity_base[1] * diffs[1][:3]
        + velocity_base[2] * diffs[2][:3]
    )
    pressure_grad = jnp.stack([diffs[0][3], diffs[1][3], diffs[2][3]])
    velocity = (source[:3] + viscous * neighbours[:3] + 0.5 * convect - 0.5 * pressure_grad) / (
        6.0 * viscous + 1.0
    )
    diverge = diffs[0][0] + diffs[1][1] + diffs[2][2]
    pressure = (source[3] + neighbours[3] - 0.5 * diverge) / 7.0
    curvature = beside_all(base_full[:3]) - 6.0 * velocity_base
    eddy_new = (
        source[4] + viscous * neighbours[4] + 0.25 * jnp.sum(centre[:3] * curvature, axis=0)
    ) / (6.0 * viscous + 2.0)
    return jnp.concatenate([velocity, pressure[None], eddy_new[None]], axis=0)


def shards(
    adjoint_start,
    adjoint_source,
    base_flow,
    eddy_visc,
    rotor_count,
    rotor_cell,
    rotor_turbine,
    rotor_sector,
    rotor_weight,
):
    base_four = jnp.concatenate([base_flow, eddy_visc[None]], axis=0)
    base_pad = extended(base_four, (("east", 1), ("north", 2)), 1)
    state = adjoint_start
    for sweep in range(2):
        state_pad = extended(state, (("east", 1), ("north", 2)), 1)
        state = relax(state_pad, base_pad, adjoint_source)
    cells = rotor_cell.reshape(-1)
    flat_state = state.reshape(5, -1)
    values = flat_state[:, cells]
    chosen = jnp.stack([values[0], values[1], values[2], values[4]])
    upstream = base_flow[0].reshape(-1)[cells]
    slot_count = cells.shape[0]
    live = jnp.arange(slot_count, dtype=jnp.int32) < rotor_count.reshape(-1)[0]
    factor = jnp.where(live, rotor_weight.reshape(-1) * upstream * jnp.abs(upstream), 0.0)
    terms = chosen * factor[None]
    sector_hot = (
        rotor_sector.reshape(-1)[None, :] == jnp.arange(SECT, dtype=jnp.int32)[:, None]
    ).astype(jnp.float32)
    combined = (terms[:, None, :] * sector_hot[None]).reshape(4 * SECT, slot_count)
    turbine_total_count = TURB_DEV * lax.axis_size("north")
    turbine_hot = (
        rotor_turbine.reshape(-1)[:, None]
        == jnp.arange(turbine_total_count, dtype=jnp.int32)[None, :]
    ).astype(jnp.float32)
    partial_grad = jnp.dot(
        combined, turbine_hot, precision=lax.Precision.HIGHEST, preferred_element_type=jnp.float32
    )
    summed = lax.psum(partial_grad, ("east", "north"))
    owned = lax.dynamic_slice_in_dim(summed, lax.axis_index("north") * TURB_DEV, TURB_DEV, 1)
    return (state, owned.reshape(4, SECT, TURB_DEV))


def solution(mesh):
    placed = (
        P(None, "east", "north", None),
        P(None, "east", "north", None),
        P(None, "east", "north", None),
        P("east", "north", None),
        P("east", "north"),
        P("east", "north", None),
        P("east", "north", None),
        P("east", "north", None),
        P("east", "north", None),
    )
    return jax.shard_map(
        shards,
        mesh=mesh,
        in_specs=placed,
        out_specs=(P(None, "east", "north", None), P(None, None, "north")),
        check_vma=False,
    )
```

profile of v0, /device:TPU:1, one launch (start us, length us, event | category | flops | bytes accessed | tf_op | source)
XLA Modules:
  0.0 241.2 jit_solution(15971372391863261522)
XLA Ops:
  0.6 1.9 pad_maximum_fusion.37
  2.5 6.3 %collective-permute-start.5 = (f32[4,1,32,256]{3,2,1,0:T(8,128)}, f32[4,1,32,256]{3,2,1,0:T(8,128)}, u32[]{:S(2)}, u32[]{:S(2)}) collective-permute-start(f32[4,1,32,256]{3,2,1,0:T(8,128)} %get-tuple-element.27), channel_id=1, source_target_pairs={{0,32},{32,64},{64,96},{96,128},{128,160},{160,192},{192,224},{1,3... | collective-permute-start | bytes 393224 | tf_op jit(solution)/shard_map/ppermute | solution.py:17
  8.8 1.9 collective-permute-start.4
  10.7 1.7 fusion.45
  12.5 1.9 collective-permute-start
  14.4 4.5 %collective-permute-start.1 = (f32[5,1,32,256]{3,2,1,0:T(8,128)}, f32[5,1,32,256]{3,2,1,0:T(8,128)S(1)}, u32[]{:S(2)}, u32[]{:S(2)}) collective-permute-start(f32[5,1,32,256]{3,2,1,0:T(8,128)} %get-tuple-element.24), channel_id=1, source_target_pairs={{0,32},{32,64},{64,96},{96,128},{128,160},{160,192},{192,224},{1,3... | collective-permute-start | bytes 491528 | tf_op jit(solution)/shard_map/ppermute | solution.py:17
  19.9 1.5 fusion.46
  22.7 1.3 copy.25
  24.0 6.2 %gather_fusion.1 = f32[1024]{0:T(1024)S(1)} fusion(f32[131072]{0:T(1024)S(1)} %bitcast.42, s32[1024]{0:T(1024)S(1)} %broadcast_clamp_fusion), kind=kCustom, calls=%fused_computation.1 | custom fusion | bytes 12288 | tf_op jit(solution)/shard_map/gather | solution.py:89
  31.2 3.1 %collective-permute-start.7 = (f32[4,18,1,256]{3,2,1,0:T(1,128)S(1)}, f32[4,18,1,256]{3,2,1,0:T(1,128)S(1)}, u32[]{:S(2)}, u32[]{:S(2)}) collective-permute-start(f32[4,18,1,256]{3,2,1,0:T(1,128)S(1)} %get-tuple-element.25), channel_id=1, source_target_pairs={{0,1},{1,2},{2,3},{3,4},{4,5},{5,6},{6,7},{7,8},{8,9},{9,10},{10,1... | collective-permute-start | bytes 221192 | tf_op jit(solution)/shard_map/ppermute | solution.py:17
  34.4 1.3 collective-permute-start.6
  36.5 4.0 %collective-permute-start.3 = (f32[5,18,1,256]{3,2,1,0:T(1,128)S(1)}, f32[5,18,1,256]{3,2,1,0:T(1,128)S(1)}, u32[]{:S(2)}, u32[]{:S(2)}) collective-permute-start(f32[5,18,1,256]{3,2,1,0:T(1,128)S(1)} %get-tuple-element.14), channel_id=1, source_target_pairs={{0,1},{1,2},{2,3},{3,4},{4,5},{5,6},{6,7},{7,8},{8,9},{9,10},{10,1... | collective-permute-start | bytes 276488 | tf_op jit(solution)/shard_map/ppermute | solution.py:17
  40.5 1.3 collective-permute-start.2
  42.6 5.5 %select_maximum_fusion.8 = f32[4,18,34,258]{3,2,1,0:T(8,128)S(1)} fusion(f32[4,18,1,256]{3,2,1,0:T(1,128)S(1)} %collective-permute-done.6, f32[4,18,1,256]{3,2,1,0:T(1,128)S(1)} %collective-permute-done.7, f32[4,1,32,256]{3,2,1,0:T(8,128)} %collective-permute-done.4, f32[4,1,32,256]{3,2,1,0:T(8,128)} %collective-permute-done.5, ...), kind=kLoop, calls=%fused_computation.15 | loop fusion | flops 8842176 | bytes 5033088 | tf_op jit(solution)/shard_map/concatenate | solution.py:19
  48.2 3.0 %select_maximum_fusion.6 = f32[5,18,34,258]{3,2,1,0:T(8,128)S(1)} fusion(f32[5,18,1,256]{3,2,1,0:T(1,128)S(1)} %collective-permute-done.2, f32[5,18,32,256]{3,2,1,0:T(8,128)S(1)} %constant_dynamic-update-slice_fusion, f32[5,18,1,256]{3,2,1,0:T(1,128)S(1)} %collective-permute-done.3), kind=kLoop, calls=%fused_computation.12 | loop fusion | flops 6315840 | bytes 6291360 | tf_op jit(solution)/shard_map/concatenate | solution.py:19
  51.3 3.6 %slice_subtract_fusion.1 = (f32[5,16,32,256]{3,2,1,0:T(8,128)S(1)}, f32[5,16,32,256]{3,2,1,0:T(8,128)S(1)}, f32[5,16,32,256]{3,2,1,0:T(8,128)S(1)}) fusion(f32[5,18,34,258]{3,2,1,0:T(8,128)S(1)} %select_maximum_fusion.6, f32[5,18,32,256]{3,2,1,0:T(8,128)S(1)} %constant_dynamic-update-slice_fusion, f32[5,18,1,256]{3,2,1,0:T(1,128)S(1)} %collective-permute-done.3, ...), kind=kLoop, calls=%fused_computation.46 | loop fusion | flops 7208960 | bytes 19189760 | tf_op jit(solution)/shard_map/sub | solution.py:37
  55.0 5.9 %multiply_reduce_fusion = (f32[16,32,256]{2,1,0:T(8,128)}, f32[16,32,256]{2,1,0:T(8,128)}, f32[3,16,32,256]{3,2,1,0:T(8,128)S(1)}) fusion(f32[5,16,32,256]{3,2,1,0:T(8,128)S(1)} %copy-done.2, f32[16,32,256]{2,1,0:T(8,128)S(1)} %copy-done.5, f32[1,16,32,256]{3,2,1,0:T(8,128)S(1)} %slice.361, f32[1,16,32,256]{3,2,1,0:T(8,128)S(1)} %slice.360, ...), kind=kLoop, calls=%fused_computation.92 | loop fusion | flops 14286848 | bytes 21905408 | tf_op jit(solution)/shard_map/reduce_sum | solution.py:63
  60.9 2.0 fusion.37
  63.0 4.7 %collective-permute-start.9 = (f32[5,1,32,256]{3,2,1,0:T(8,128)S(1)}, f32[5,1,32,256]{3,2,1,0:T(8,128)S(1)}, u32[]{:S(2)}, u32[]{:S(2)}) collective-permute-start(f32[5,1,32,256]{3,2,1,0:T(8,128)S(1)} %get-tuple-element.19), channel_id=1, source_target_pairs={{0,32},{32,64},{64,96},{96,128},{128,160},{160,192},{192,224},{1,3... | collective-permute-start | bytes 491528 | tf_op jit(solution)/shard_map/ppermute | solution.py:17
  67.7 1.9 collective-permute-start.8
  70.0 5.7 %collective-permute-done.8 = f32[5,1,32,256]{3,2,1,0:T(8,128)S(1)} collective-permute-done((f32[5,1,32,256]{3,2,1,0:T(8,128)S(1)}, f32[5,1,32,256]{3,2,1,0:T(8,128)S(1)}, u32[]{:S(2)}, u32[]{:S(2)}) %collective-permute-start.8) | collective-permute-done | bytes 163872 | tf_op jit(solution)/shard_map/ppermute | solution.py:18
  75.8 5.7 %collective-permute-start.11 = (f32[5,18,1,256]{3,2,1,0:T(1,128)S(1)}, f32[5,18,1,256]{3,2,1,0:T(1,128)S(1)}, u32[]{:S(2)}, u32[]{:S(2)}) collective-permute-start(f32[5,18,1,256]{3,2,1,0:T(1,128)S(1)} %get-tuple-element.12), channel_id=1, source_target_pairs={{0,1},{1,2},{2,3},{3,4},{4,5},{5,6},{6,7},{7,8},{8,9},{9,10},{10,1... | collective-permute-start | bytes 276488 | tf_op jit(solution)/shard_map/ppermute | solution.py:17
  83.3 3.5 %collective-permute-done.10 = f32[5,18,1,256]{3,2,1,0:T(1,128)S(1)} collective-permute-done((f32[5,18,1,256]{3,2,1,0:T(1,128)S(1)}, f32[5,18,1,256]{3,2,1,0:T(1,128)S(1)}, u32[]{:S(2)}, u32[]{:S(2)}) %collective-permute-start.10) | collective-permute-done | bytes 92192 | tf_op jit(solution)/shard_map/ppermute | solution.py:18
  86.8 6.1 %select_maximum_fusion = f32[5,18,34,258]{3,2,1,0:T(8,128)S(1)} fusion(f32[5,18,1,256]{3,2,1,0:T(1,128)S(1)} %collective-permute-done.10, f32[5,18,1,256]{3,2,1,0:T(1,128)S(1)} %collective-permute-done.11, f32[5,1,32,256]{3,2,1,0:T(8,128)S(1)} %collective-permute-done.8, f32[5,1,32,256]{3,2,1,0:T(8,128)S(1)} %collective-permute-done.9, ...), kind=kLoop, calls=%fused_computation.6 | loop fusion | flops 12631680 | bytes 6291360 | tf_op jit(solution)/shard_map/concatenate | solution.py:19
  95.0 4.5 %add_add_fusion = f32[5,16,32,256]{3,2,1,0:T(8,128)S(1)} fusion(f32[5,18,34,258]{3,2,1,0:T(8,128)S(1)} %select_maximum_fusion, f32[5,1,32,256]{3,2,1,0:T(8,128)S(1)} %collective-permute-done.8, f32[1,16,32,256]{3,2,1,0:T(8,128)S(1)} %get-tuple-element.10, f32[1,16,32,256]{3,2,1,0:T(8,128)S(1)} %get-tuple-element.9, ...), kind=kLoop, calls=%fused_computation.43 | loop fusion | flops 13762560 | bytes 10997760 | tf_op jit(solution)/shard_map/add | solution.py:30
  101.4 1.5 fusion.8
  102.8 1.8 pad_maximum_fusion.21
  105.7 3.3 %pad_maximum_fusion = f32[5,131072]{1,0:T(8,128)} fusion(f32[1,131072]{1,0:T(1,128)S(1)} %bitcast.53, f32[1,131072]{1,0:T(1,128)S(1)} %bitcast.54, f32[3,131072]{1,0:T(4,128)S(1)} %bitcast.48), kind=kLoop, calls=%fused_computation.21 | loop fusion | flops 1310720 | bytes 5242880 | tf_op jit(solution)/shard_map/concatenate | solution.py:65
  109.0 30.3 %copy.18 = f32[5,131072]{0,1:T(8,128)} copy(f32[5,131072]{1,0:T(8,128)} %pad_maximum_fusion) | data formatting | bytes 5242880 | tf_op jit(solution)/shard_map/concatenate | solution.py:65
  139.3 10.7 %gather_fusion = f32[1024,5]{1,0:T(8,128)S(1)} fusion(f32[5,131072]{0,1:T(8,128)} %copy.18, s32[1024]{0:T(1024)S(1)} %broadcast_clamp_fusion), kind=kCustom, calls=%fused_computation | custom fusion | bytes 45056 | tf_op jit(solution)/shard_map/gather | solution.py:87
  150.6 1.6 fusion.22
  152.2 88.3 %psum.7 = f32[32,384]{0,1:T(8,128)S(1)} all-reduce(f32[32,384]{0,1:T(8,128)S(1)} %fusion.22), channel_id=1, replica_groups=mesh['east'=8,'north'=32] {'east','north'}, use_global_device_ids=true, to_apply=%region_2.3 | all-reduce | flops 12288 | bytes 98304 | tf_op jit(solution)/shard_map/psum | solution.py:106
  (71 shorter events, 12.8 us)
Async XLA Ops:
  0.6 19.3 %copy-start = (f32[3,16,32,256]{3,2,1,0:T(8,128)S(1)}, f32[3,16,32,256]{3,2,1,0:T(8,128)}, u32[]{:S(2)}) copy-start(f32[3,16,32,256]{3,2,1,0:T(8,128)} %param.11) | copy-start | bytes 4718596
  0.6 18.3 %copy-start.1 = (f32[16,32,256]{2,1,0:T(8,128)S(1)}, f32[16,32,256]{2,1,0:T(8,128)}, u32[]{:S(2)}) copy-start(f32[16,32,256]{2,1,0:T(8,128)} %param.12) | copy-start | bytes 1572868
  2.5 27.6 %collective-permute-start.5 = (f32[4,1,32,256]{3,2,1,0:T(8,128)}, f32[4,1,32,256]{3,2,1,0:T(8,128)}, u32[]{:S(2)}, u32[]{:S(2)}) collective-permute-start(f32[4,1,32,256]{3,2,1,0:T(8,128)} %get-tuple-element.27), channel_id=1, source_target_pairs={{0,32},{32,64},{64,96},{96,128},{128,160},{160,192},{192,224},{1,3... | collective-permute-start | bytes 393224 | tf_op jit(solution)/shard_map/ppermute | solution.py:17
  8.8 21.4 %collective-permute-start.4 = (f32[4,1,32,256]{3,2,1,0:T(8,128)}, f32[4,1,32,256]{3,2,1,0:T(8,128)}, u32[]{:S(2)}, u32[]{:S(2)}) collective-permute-start(f32[4,1,32,256]{3,2,1,0:T(8,128)} %get-tuple-element.28), channel_id=1, source_target_pairs={{32,0},{64,32},{96,64},{128,96},{160,128},{192,160},{224,192},{33,... | collective-permute-start | bytes 393224 | tf_op jit(solution)/shard_map/ppermute | solution.py:18
  12.5 23.2 %collective-permute-start = (f32[5,1,32,256]{3,2,1,0:T(8,128)}, f32[5,1,32,256]{3,2,1,0:T(8,128)S(1)}, u32[]{:S(2)}, u32[]{:S(2)}) collective-permute-start(f32[5,1,32,256]{3,2,1,0:T(8,128)} %get-tuple-element.23), channel_id=1, source_target_pairs={{32,0},{64,32},{96,64},{128,96},{160,128},{192,160},{224,192},{33,... | collective-permute-start | bytes 491528 | tf_op jit(solution)/shard_map/ppermute | solution.py:18
  14.4 7.0 %copy-start.14 = (s32[1,1,1024]{2,1,0:T(1,128)S(1)}, s32[1,1,1024]{2,1,0:T(1,128)}, u32[]{:S(2)}) copy-start(s32[1,1,1024]{2,1,0:T(1,128)} %param.14) | copy-start | bytes 12292
  14.4 7.0 %copy-start.12 = (s32[1,1,1024]{2,1,0:T(1,128)S(1)}, s32[1,1,1024]{2,1,0:T(1,128)}, u32[]{:S(2)}) copy-start(s32[1,1,1024]{2,1,0:T(1,128)} %param.16) | copy-start | bytes 12292
  14.4 21.3 %collective-permute-start.1 = (f32[5,1,32,256]{3,2,1,0:T(8,128)}, f32[5,1,32,256]{3,2,1,0:T(8,128)S(1)}, u32[]{:S(2)}, u32[]{:S(2)}) collective-permute-start(f32[5,1,32,256]{3,2,1,0:T(8,128)} %get-tuple-element.24), channel_id=1, source_target_pairs={{0,32},{32,64},{64,96},{96,128},{128,160},{160,192},{192,224},{1,3... | collective-permute-start | bytes 491528 | tf_op jit(solution)/shard_map/ppermute | solution.py:17
  30.1 5.6 %copy-start.2 = (f32[5,16,32,256]{3,2,1,0:T(8,128)S(1)}, f32[5,16,32,256]{3,2,1,0:T(8,128)}, u32[]{:S(2)}) copy-start(f32[5,16,32,256]{3,2,1,0:T(8,128)} %param.9) | copy-start | bytes 7864324
  31.2 11.4 %collective-permute-start.7 = (f32[4,18,1,256]{3,2,1,0:T(1,128)S(1)}, f32[4,18,1,256]{3,2,1,0:T(1,128)S(1)}, u32[]{:S(2)}, u32[]{:S(2)}) collective-permute-start(f32[4,18,1,256]{3,2,1,0:T(1,128)S(1)} %get-tuple-element.25), channel_id=1, source_target_pairs={{0,1},{1,2},{2,3},{3,4},{4,5},{5,6},{6,7},{7,8},{8,9},{9,10},{10,1... | collective-permute-start | bytes 221192 | tf_op jit(solution)/shard_map/ppermute | solution.py:17
  34.4 8.3 %collective-permute-start.6 = (f32[4,18,1,256]{3,2,1,0:T(1,128)S(1)}, f32[4,18,1,256]{3,2,1,0:T(1,128)S(1)}, u32[]{:S(2)}, u32[]{:S(2)}) collective-permute-start(f32[4,18,1,256]{3,2,1,0:T(1,128)S(1)} %get-tuple-element.26), channel_id=1, source_target_pairs={{1,0},{2,1},{3,2},{4,3},{5,4},{6,5},{7,6},{8,7},{9,8},{10,9},{11,1... | collective-permute-start | bytes 221192 | tf_op jit(solution)/shard_map/ppermute | solution.py:18
  36.3 11.8 %copy-start.3 = (f32[5,16,32,256]{3,2,1,0:T(8,128)}, f32[5,16,32,256]{3,2,1,0:T(8,128)S(1)}, u32[]{:S(2)}) copy-start(f32[5,16,32,256]{3,2,1,0:T(8,128)S(1)} %get-tuple-element.21) | copy-start | bytes 7864324
  36.5 11.7 %collective-permute-start.3 = (f32[5,18,1,256]{3,2,1,0:T(1,128)S(1)}, f32[5,18,1,256]{3,2,1,0:T(1,128)S(1)}, u32[]{:S(2)}, u32[]{:S(2)}) collective-permute-start(f32[5,18,1,256]{3,2,1,0:T(1,128)S(1)} %get-tuple-element.14), channel_id=1, source_target_pairs={{0,1},{1,2},{2,3},{3,4},{4,5},{5,6},{6,7},{7,8},{8,9},{9,10},{10,1... | collective-permute-start | bytes 276488 | tf_op jit(solution)/shard_map/ppermute | solution.py:17
  40.5 7.7 %collective-permute-start.2 = (f32[5,18,1,256]{3,2,1,0:T(1,128)S(1)}, f32[5,18,1,256]{3,2,1,0:T(1,128)S(1)}, u32[]{:S(2)}, u32[]{:S(2)}) collective-permute-start(f32[5,18,1,256]{3,2,1,0:T(1,128)S(1)} %get-tuple-element.15), channel_id=1, source_target_pairs={{1,0},{2,1},{3,2},{4,3},{5,4},{6,5},{7,6},{8,7},{9,8},{10,9},{11,1... | collective-permute-start | bytes 276488 | tf_op jit(solution)/shard_map/ppermute | solution.py:18
  42.6 5.5 %copy-start.10 = (f32[4,18,1,256]{3,2,1,0:T(1,128)}, f32[4,18,1,256]{3,2,1,0:T(1,128)S(1)}, u32[]{:S(2)}) copy-start(f32[4,18,1,256]{3,2,1,0:T(1,128)S(1)} %collective-permute-done.6) | copy-start | bytes 221188
  51.2 3.7 %copy-start.5 = (f32[16,32,256]{2,1,0:T(8,128)S(1)}, f32[16,32,256]{2,1,0:T(8,128)}, u32[]{:S(2)}) copy-start(f32[16,32,256]{2,1,0:T(8,128)} %get-tuple-element.34) | copy-start | bytes 1572868
  51.2 3.7 %copy-start.6 = (f32[16,32,256]{2,1,0:T(8,128)S(1)}, f32[16,32,256]{2,1,0:T(8,128)}, u32[]{:S(2)}) copy-start(f32[16,32,256]{2,1,0:T(8,128)} %get-tuple-element.30) | copy-start | bytes 1572868
  51.2 3.7 %copy-start.7 = (f32[16,32,256]{2,1,0:T(8,128)S(1)}, f32[16,32,256]{2,1,0:T(8,128)}, u32[]{:S(2)}) copy-start(f32[16,32,256]{2,1,0:T(8,128)} %get-tuple-element.31) | copy-start | bytes 1572868
  63.0 6.7 %copy-start.13 = (f32[1,1,1024]{2,1,0:T(1,128)S(1)}, f32[1,1,1024]{2,1,0:T(1,128)}, u32[]{:S(2)}) copy-start(f32[1,1,1024]{2,1,0:T(1,128)} %param.17) | copy-start | bytes 12292
  63.0 7.0 %collective-permute-start.9 = (f32[5,1,32,256]{3,2,1,0:T(8,128)S(1)}, f32[5,1,32,256]{3,2,1,0:T(8,128)S(1)}, u32[]{:S(2)}, u32[]{:S(2)}) collective-permute-start(f32[5,1,32,256]{3,2,1,0:T(8,128)S(1)} %get-tuple-element.19), channel_id=1, source_target_pairs={{0,32},{32,64},{64,96},{96,128},{128,160},{160,192},{192,224},{1,3... | collective-permute-start | bytes 491528 | tf_op jit(solution)/shard_map/ppermute | solution.py:17
  67.7 7.9 %collective-permute-start.8 = (f32[5,1,32,256]{3,2,1,0:T(8,128)S(1)}, f32[5,1,32,256]{3,2,1,0:T(8,128)S(1)}, u32[]{:S(2)}, u32[]{:S(2)}) collective-permute-start(f32[5,1,32,256]{3,2,1,0:T(8,128)S(1)} %get-tuple-element.20), channel_id=1, source_target_pairs={{32,0},{64,32},{96,64},{128,96},{160,128},{192,160},{224,192},{33,... | collective-permute-start | bytes 491528 | tf_op jit(solution)/shard_map/ppermute | solution.py:18
  75.8 7.5 %collective-permute-start.11 = (f32[5,18,1,256]{3,2,1,0:T(1,128)S(1)}, f32[5,18,1,256]{3,2,1,0:T(1,128)S(1)}, u32[]{:S(2)}, u32[]{:S(2)}) collective-permute-start(f32[5,18,1,256]{3,2,1,0:T(1,128)S(1)} %get-tuple-element.12), channel_id=1, source_target_pairs={{0,1},{1,2},{2,3},{3,4},{4,5},{5,6},{6,7},{7,8},{8,9},{9,10},{10,1... | collective-permute-start | bytes 276488 | tf_op jit(solution)/shard_map/ppermute | solution.py:17
  81.5 5.3 %collective-permute-start.10 = (f32[5,18,1,256]{3,2,1,0:T(1,128)S(1)}, f32[5,18,1,256]{3,2,1,0:T(1,128)S(1)}, u32[]{:S(2)}, u32[]{:S(2)}) collective-permute-start(f32[5,18,1,256]{3,2,1,0:T(1,128)S(1)} %get-tuple-element.13), channel_id=1, source_target_pairs={{1,0},{2,1},{3,2},{4,3},{5,4},{6,5},{7,6},{8,7},{9,8},{10,9},{11,1... | collective-permute-start | bytes 276488 | tf_op jit(solution)/shard_map/ppermute | solution.py:18
  95.0 4.6 %copy-start.4 = (f32[5,16,32,256]{3,2,1,0:T(8,128)S(1)}, f32[5,16,32,256]{3,2,1,0:T(8,128)}, u32[]{:S(2)}) copy-start(f32[5,16,32,256]{3,2,1,0:T(8,128)} %param.10) | copy-start | bytes 7864324
  95.0 4.6 %copy-start.9 = (f32[16,32,256]{2,1,0:T(8,128)S(1)}, f32[16,32,256]{2,1,0:T(8,128)}, u32[]{:S(2)}) copy-start(f32[16,32,256]{2,1,0:T(8,128)} %get-tuple-element.2) | copy-start | bytes 1572868
  99.5 1.8 copy-start.8
  109.0 41.6 %copy-start.11 = (f32[8,1024]{1,0:T(8,128)S(1)}, f32[8,1024]{1,0:T(8,128)}, u32[]{:S(2)}) copy-start(f32[8,1024]{1,0:T(8,128)} %fusion.42) | copy-start | bytes 98308
  109.0 41.6 %copy-start.15 = (s32[1,1,1024]{2,1,0:T(1,128)S(1)}, s32[1,1,1024]{2,1,0:T(1,128)}, u32[]{:S(2)}) copy-start(s32[1,1,1024]{2,1,0:T(1,128)} %param.15) | copy-start | bytes 12292
where the time goes:
time: 242 us; the launch traced here: 241 us
  blocking collectives  88.3 us (36%)
  local copies, waits for them, and re-layouts  56.2 us (23%)
  other arithmetic  45.7 us (19%)
  starting transfers between devices  38 us (16%)
  waiting for transfers between devices  9.52 us (4%)
    psum x1, blocking collectives, shards(): summed = lax.psum(partial_grad, ('east', 'north'))  88.3 us
    concatenate x1, local copies, waits for them, and re-layouts, relax(): return jnp.concatenate([velocity, pressure[None], eddy_new[None]], axis=0)  30.3 us
    ppermute x6, starting transfers between devices, extended(): before = lax.ppermute(last, axis, up)  28.4 us
    concatenate x5, other arithmetic, extended(): shard = jnp.concatenate([before, shard, after], axis=dim)  15.8 us
    gather x1, local copies, waits for them, and re-layouts, shards(): values = flat_state[:, cells]  10.7 us
    ppermute x6, starting transfers between devices, extended(): after = lax.ppermute(leading, axis, down)  9.63 us
    ppermute x6, waiting for transfers between devices, extended(): after = lax.ppermute(leading, axis, down)  9.21 us
    gather x1, local copies, waits for them, and re-layouts, shards(): upstream = base_flow[0].reshape(-1)[cells]  6.15 us
  transfers between devices with their start and end apart: 12, of which 3 were waited for; matrix products, arithmetic and copies ran while one was open for 9% of the time, Pallas kernels for 0%

commit v1 on v0

v1 whole, which is shorter than its diff:
```python
import functools

import jax
import jax.numpy as jnp
from jax import lax
from jax.experimental import pallas as pl
from jax.experimental.pallas import tpu as pltpu
from jax.sharding import PartitionSpec as P

SECT = 8
TURB_DEV = 12
PITCH = 16
PAD = 8
MESH = pl.DeviceIdType.MESH
F32, BF16, I32 = jnp.float32, jnp.bfloat16, jnp.int32

VQ, EDDY, BASE = 0, 1, 2
EAST_UP, EAST_DOWN, NORTH_UP, NORTH_DOWN = 0, 1, 2, 3


def split(x):
    high = x.astype(BF16)
    return high, (x - high.astype(F32)).astype(BF16)


def kernel(
    n_east,
    n_north,
    start,
    source,
    base,
    eddy,
    count,
    cell,
    turbine,
    sector,
    weight,
    final,
    grad,
    v0,
    v1,
    v2,
    flow,
    visc,
    src,
    coef,
    rest,
    curve,
    levels,
    parts,
    gathered,
    totals,
    load_sem,
    out_sem,
    send_sem,
    recv_sem,
    part_send,
    part_recv,
    total_send,
    total_recv,
):
    _, ce, cn, cz = start.shape
    slots = cell.shape[-1]
    east, north = lax.axis_index("east"), lax.axis_index("north")
    rows, planes = pl.ds(PAD, cn), pl.ds(1, ce)

    loads = [
        pltpu.make_async_copy(eddy, visc, load_sem.at[0]),
        pltpu.make_async_copy(base, flow.at[:, planes, rows, :], load_sem.at[1]),
        pltpu.make_async_copy(start.at[0:4], v0.at[0:4, planes, rows, :], load_sem.at[2]),
        pltpu.make_async_copy(source, src, load_sem.at[3]),
        pltpu.make_async_copy(start.at[4:5], v0.at[4:5, planes, rows, :], load_sem.at[4]),
    ]
    for load in loads:
        load.start()

    barrier = pltpu.get_barrier_semaphore()

    def greet_north(k, carry):
        pl.semaphore_signal(barrier, inc=1, device_id={"north": lax.rem(north + k, n_north)}, device_id_type=MESH)
        return carry

    def greet_east(k, carry):
        pl.semaphore_signal(barrier, inc=1, device_id={"east": lax.rem(east + k, n_east)}, device_id_type=MESH)
        return carry

    lax.fori_loop(1, n_north, greet_north, 0)
    lax.fori_loop(1, n_east, greet_east, 0)

    def clear(at_end, plane, row):
        @pl.when(at_end)
        def _():
            for ref in (v0, v1, flow):
                if row is None:
                    ref[:, plane, rows, :] = jnp.zeros((ref.shape[0], cn, cz), F32)
                else:
                    ref[:, planes, row : row + 1, :] = jnp.zeros((ref.shape[0], ce, 1, cz), F32)

    clear(east == 0, 0, None)
    clear(east == n_east - 1, ce + 1, None)
    clear(north == 0, None, PAD - 1)
    clear(north == n_north - 1, None, PAD + cn)

    pl.semaphore_wait(barrier, n_north + n_east - 2)

    def halo(sweep, group, sent, landing, fields, padded):
        first, last = (1, ce) if padded else (0, ce - 1)
        low, high = (PAD, PAD + cn - 1) if padded else (0, cn - 1)
        row_all = rows if padded else slice(None)
        plane_all = planes if padded else slice(None)
        ends = [
            (
                sent.at[fields, last, row_all, :],
                landing.at[fields, 0, rows, :],
                {"east": east + 1},
                east < n_east - 1,
                east > 0,
            ),
            (
                sent.at[fields, first, row_all, :],
                landing.at[fields, ce + 1, rows, :],
                {"east": east - 1},
                east > 0,
                east < n_east - 1,
            ),
            (
                sent.at[fields, plane_all, high : high + 1, :],
                landing.at[fields, planes, PAD - 1 : PAD, :],
                {"north": north + 1},
                north < n_north - 1,
                north > 0,
            ),
            (
                sent.at[fields, plane_all, low : low + 1, :],
                landing.at[fields, planes, PAD + cn : PAD + cn + 1, :],
                {"north": north - 1},
                north > 0,
                north < n_north - 1,
            ),
        ]
        return [
            (
                pltpu.make_async_remote_copy(
                    src_ref=a,
                    dst_ref=b,
                    send_sem=send_sem.at[sweep, group, side],
                    recv_sem=recv_sem.at[sweep, group, side],
                    device_id=target,
                    device_id_type=MESH,
                ),
                sends,
                gets,
            )
            for side, (a, b, target, sends, gets) in enumerate(ends)
        ]

    def begin(copy, sends, gets):
        @pl.when(sends)
        def _():
            copy.start()

    def landed(copy, sends, gets):
        @pl.when(gets)
        def _():
            copy.wait_recv()

    def left(copy, sends, gets):
        @pl.when(sends)
        def _():
            copy.wait_send()

    first_vq = halo(0, VQ, start, v0, slice(0, 4), False)
    first_eddy = halo(0, EDDY, start, v0, slice(4, 5), False)
    first_base = halo(0, BASE, base, flow, slice(0, 3), False)
    second_vq = halo(1, VQ, v1, v1, slice(0, 4), True)
    second_eddy = halo(1, EDDY, v1, v1, slice(4, 5), True)

    for group in (first_vq, first_base, first_eddy):
        for copy in group:
            begin(*copy)

    lane = lax.broadcasted_iota(I32, (cn, cz), 1)
    top, bottom = lane == cz - 1, lane == 0

    for load in loads[:2]:
        load.wait()

    def prepare(e, carry):
        w = 1.0 + visc[e]
        r1 = 1.0 / (6.0 * w + 1.0)
        half = 0.5 * r1
        wr = w * r1
        for k in range(3):
            hu = half * flow[k, e + 1, rows, :]
            above, below = wr + hu, wr - hu
            if k == 2:
                above, below = jnp.where(top, 0.0, above), jnp.where(bottom, 0.0, below)
            coef[2 * k, e] = above
            coef[2 * k + 1, e] = below
        coef[6, e] = half
        r2 = 1.0 / (6.0 * w + 2.0)
        rest[0, e] = r2
        rest[1, e] = w * r2
        return carry

    lax.fori_loop(0, ce, prepare, 0)

    entry_cell = cell[0]
    row_of = lax.shift_right_logical(entry_cell, cz.bit_length() - 1)
    level_of = lax.bitwise_and(entry_cell, cz - 1)
    levels[...] = jnp.where(lax.broadcasted_iota(I32, (cz, slots), 0) == level_of, 1.0, 0.0).astype(BF16)
    step = 4
    block_rows = step * cn
    row_iota = lax.broadcasted_iota(I32, (block_rows, slots), 0)

    def gather(read):
        def block(p, acc):
            high, low = split(read(p * step).reshape(block_rows, cz))
            hot = levels[...]
            found = jnp.dot(high, hot, preferred_element_type=F32) + jnp.dot(low, hot, preferred_element_type=F32)
            kept = jnp.where(row_iota == row_of - p * block_rows, found, 0.0)
            return acc + jnp.sum(kept.reshape(block_rows // 8, 8, slots), axis=0)

        acc = lax.fori_loop(0, ce // step, block, jnp.zeros((8, slots), F32))
        return jnp.sum(acc, axis=0, keepdims=True)

    upstream = gather(lambda p: flow[0, pl.ds(p + 1, step), rows, :])
    live = lax.broadcasted_iota(I32, (1, slots), 1) < count[0, 0]
    factor = jnp.where(live, weight[0] * upstream * jnp.abs(upstream), 0.0)

    def shifted(x):
        return pltpu.roll(x, cz - 1, 1), pltpu.roll(x, 1, 1)

    def relax_vq(e, old, new, offset, where_rows):
        def beside(c):
            x = old[c, e + 1, rows, :]
            return (
                x,
                old[c, e + 2, rows, :],
                old[c, e, rows, :],
                old[c, e + 1, pl.ds(PAD + 1, cn), :],
                old[c, e + 1, pl.ds(PAD - 1, cn), :],
                *shifted(x),
            )

        _, qe, qw, qn, qs, qu, qd = beside(3)
        qu, qd = jnp.where(top, 0.0, qu), jnp.where(bottom, 0.0, qd)
        grads = (qe - qw, qn - qs, qu - qd)
        sum_q = qe + qw + qn + qs + qu + qd
        half = coef[6, e]
        r1 = half + half
        diverge = None
        for c in range(3):
            _, *near = beside(c)
            total = r1 * src[c, e] - half * grads[c]
            for k in range(6):
                total = total + coef[k, e] * near[k]
            new[c, e + offset, where_rows, :] = total
            above, below = near[2 * c], near[2 * c + 1]
            if c == 2:
                above, below = jnp.where(top, 0.0, above), jnp.where(bottom, 0.0, below)
            slope = above - below
            diverge = slope if diverge is None else diverge + slope
        new[3, e + offset, where_rows, :] = (src[3, e] + sum_q - 0.5 * diverge) * (1.0 / 7.0)

    def around(ref, c, e):
        x = ref[c, e + 1, rows, :]
        up, down = shifted(x)
        up, down = jnp.where(top, 0.0, up), jnp.where(bottom, 0.0, down)
        total = ref[c, e + 2, rows, :] + ref[c, e, rows, :]
        total = total + ref[c, e + 1, pl.ds(PAD + 1, cn), :] + ref[c, e + 1, pl.ds(PAD - 1, cn), :]
        return total + up + down, x

    def relax_eddy(e, old, new, offset, where_rows, first):
        sum_m, _ = around(old, 4, e)
        total = rest[0, e] * src[4, e] + rest[1, e] * sum_m
        turn = None
        for c in range(3):
            if first:
                sum_u, u = around(flow, c, e)
                bend = (0.25 * rest[0, e]) * (sum_u - 6.0 * u)
                curve[c, e] = bend
            else:
                bend = curve[c, e]
            total = total + old[c, e + 1, rows, :] * bend
        new[4, e + offset, where_rows, :] = total

    def inner(body):
        def step_body(e, carry):
            body(e)
            return carry

        lax.fori_loop(1, ce - 1, step_body, 0)

    for load in loads[2:]:
        load.wait()
    for copy in first_vq[2:]:
        landed(*copy)
    sweep_one = lambda e: relax_vq(e, v0, v1, 1, rows)
    inner(sweep_one)
    for copy in first_vq[:2]:
        landed(*copy)
    sweep_one(0)
    sweep_one(ce - 1)
    for copy in second_vq:
        begin(*copy)

    for group in (first_base, first_eddy):
        for copy in group:
            landed(*copy)
    eddy_one = lambda e: relax_eddy(e, v0, v1, 1, rows, True)

    def every(body):
        def step_body(e, carry):
            body(e)
            return carry

        lax.fori_loop(0, ce, step_body, 0)

    every(eddy_one)
    for copy in second_eddy:
        begin(*copy)

    for copy in second_vq[2:]:
        landed(*copy)
    sweep_two = lambda e: relax_vq(e, v1, v2, 0, slice(None))
    inner(sweep_two)
    for copy in second_vq[:2]:
        landed(*copy)
    sweep_two(0)
    sweep_two(ce - 1)
    stores = [
        pltpu.make_async_copy(v2.at[0:4], final.at[0:4], out_sem.at[0]),
        pltpu.make_async_copy(v2.at[4:5], final.at[4:5], out_sem.at[1]),
    ]
    stores[0].start()
    for copy in second_eddy:
        landed(*copy)
    every(lambda e: relax_eddy(e, v1, v2, 0, slice(None), False))
    stores[1].start()

    values = [gather(lambda p, c=c: v2[c, pl.ds(p, step), :, :]) * factor for c in (0, 1, 2, 4)]
    terms = jnp.concatenate(values + [jnp.zeros((4, slots), F32)], axis=0)
    turbine_of = turbine[0]
    owner_of = lax.shift_right_logical(turbine_of * 5462, 16)
    place_of = sector[0] * PITCH + turbine_of - owner_of * TURB_DEV
    place_hot = jnp.where(lax.broadcasted_iota(I32, (SECT * PITCH, slots), 0) == place_of, 1.0, 0.0).astype(BF16)
    owner_iota = lax.broadcasted_iota(I32, (n_north, 8, slots), 0)
    spread = jnp.where(owner_iota == owner_of[None], terms[None], 0.0).reshape(n_north * 8, slots)
    high, low = split(spread)
    contract = (((1,), (1,)), ((), ()))
    summed = lax.dot_general(high, place_hot, contract, preferred_element_type=F32)
    summed = summed + lax.dot_general(low, place_hot, contract, preferred_element_type=F32)
    parts[...] = summed.reshape(n_north, 8, SECT * PITCH)

    def part_copy(k):
        to = lax.rem(north + k, n_north)
        return pltpu.make_async_remote_copy(
            src_ref=parts.at[to],
            dst_ref=gathered.at[north],
            send_sem=part_send.at[k],
            recv_sem=part_recv.at[k],
            device_id={"north": to},
            device_id_type=MESH,
        )

    def total_copy(k):
        to = lax.rem(east + k, n_east)
        return pltpu.make_async_remote_copy(
            src_ref=totals.at[east],
            dst_ref=totals.at[east],
            send_sem=total_send.at[k],
            recv_sem=total_recv.at[k],
            device_id={"east": to},
            device_id_type=MESH,
        )

    def each(copy_of, act, size):
        def body(k, carry):
            act(copy_of(k))
            return carry

        lax.fori_loop(1, size, body, 0)

    each(part_copy, lambda c: c.start(), n_north)
    gathered[north] = parts[north]
    each(part_copy, lambda c: c.wait_recv(), n_north)
    totals[east] = jnp.sum(gathered[...], axis=0)
    each(total_copy, lambda c: c.start(), n_east)
    each(total_copy, lambda c: c.wait_recv(), n_east)
    whole = jnp.sum(totals[...], axis=0)
    for s in range(SECT):
        cut = whole[:, s * PITCH : s * PITCH + TURB_DEV]
        for c in range(4):
            grad[c, s : s + 1, :] = cut[c : c + 1]

    each(part_copy, lambda c: c.wait_send(), n_north)
    each(total_copy, lambda c: c.wait_send(), n_east)
    for group in (first_vq, first_base, first_eddy, second_vq, second_eddy):
        for copy in group:
            left(*copy)
    for store in stores:
        store.wait()


def shards(n_east, n_north, *arrays):
    start, source, base, eddy, count, cell = arrays[:6]
    _, ce, cn, cz = start.shape
    slots = cell.shape[-1]
    padded = (ce + 2, cn + 2 * PAD, cz)
    hbm, vmem = pl.BlockSpec(memory_space=pl.ANY), pl.BlockSpec(memory_space=pltpu.VMEM)
    return tuple(
        pl.pallas_call(
            functools.partial(kernel, n_east, n_north),
            out_shape=(
                jax.ShapeDtypeStruct(start.shape, F32),
                jax.ShapeDtypeStruct((4, SECT, TURB_DEV), F32),
            ),
            in_specs=[hbm] * 4 + [pl.BlockSpec(memory_space=pltpu.SMEM)] + [vmem] * 4,
            out_specs=(hbm, vmem),
            scratch_shapes=[
                pltpu.VMEM((5, *padded), F32),
                pltpu.VMEM((5, *padded), F32),
                pltpu.VMEM((5, ce, cn, cz), F32),
                pltpu.VMEM((3, *padded), F32),
                pltpu.VMEM((ce, cn, cz), F32),
                pltpu.VMEM((5, ce, cn, cz), F32),
                pltpu.VMEM((7, ce, cn, cz), F32),
                pltpu.VMEM((2, ce, cn, cz), F32),
                pltpu.VMEM((3, ce, cn, cz), F32),
                pltpu.VMEM((cz, slots), BF16),
                pltpu.VMEM((n_north, 8, SECT * PITCH), F32),
                pltpu.VMEM((n_north, 8, SECT * PITCH), F32),
                pltpu.VMEM((n_east, 8, SECT * PITCH), F32),
                pltpu.SemaphoreType.DMA((5,)),
                pltpu.SemaphoreType.DMA((2,)),
                pltpu.SemaphoreType.DMA((2, 3, 4)),
                pltpu.SemaphoreType.DMA((2, 3, 4)),
                pltpu.SemaphoreType.DMA((n_north,)),
                pltpu.SemaphoreType.DMA((n_north,)),
                pltpu.SemaphoreType.DMA((n_east,)),
                pltpu.SemaphoreType.DMA((n_east,)),
            ],
            compiler_params=pltpu.CompilerParams(
                collective_id=0, has_side_effects=True, vmem_limit_bytes=56 * 1024 * 1024
            ),
        )(*arrays)
    )


def solution(mesh):
    fields, scalars = P(None, "east", "north", None), P("east", "north", None)
    return jax.shard_map(
        functools.partial(shards, mesh.shape["east"], mesh.shape["north"]),
        mesh=mesh,
        in_specs=(fields, fields, fields, scalars, P("east", "north"), scalars, scalars, scalars, scalars),
        out_specs=(fields, P(None, None, "north")),
        check_vma=False,
    )
```

time: 242 us -> 55.3 us (0.23)
  blocking collectives: 88.3 us -> 0 us
  local copies, waits for them, and re-layouts: 56.2 us -> 4.18 us
  Pallas kernels: 0 us -> 49.7 us
  other arithmetic: 45.7 us -> 0 us
  starting transfers between devices: 38 us -> 0 us
  waiting for transfers between devices: 9.52 us -> 0 us
    psum x1 -> x0, blocking collectives: 88.3 us -> none  [shards(): summed = lax.psum(partial_grad, ('east', 'north'))]
    pallas_call x0 -> x1, Pallas kernels: none -> 49.7 us  [shards(): pl.pallas_call(functools.partial(kernel, n_east, n_north), out_shape=(jax...]
    ppermute x12 -> x0, starting transfers between devices: 38 us -> none  [the longest x6 28.4 us: extended(): before = lax.ppermute(last, axis, up)]
    concatenate x2 -> x0, local copies, waits for them, and re-layouts: 30.3 us -> none  [the longest x1 30.3 us: relax(): return jnp.concatenate([velocity, pressure[None], eddy_new[None]], axis=0)]
    concatenate x9 -> x0, other arithmetic: 22.8 us -> none  [the longest x5 15.8 us: extended(): shard = jnp.concatenate([before, shard, after], axis=dim)]
    gather x2 -> x0, local copies, waits for them, and re-layouts: 16.8 us -> none  [the longest x1 10.7 us: shards(): values = flat_state[:, cells]]
    ppermute x12 -> x0, waiting for transfers between devices: 9.52 us -> none  [the longest x6 9.21 us: extended(): after = lax.ppermute(leading, axis, down)]
    sub x5 -> x0, other arithmetic: 6.69 us -> none  [the longest x2 4.44 us: slopes(): padded[:, 1:-1, 1:-1, 2:] - padded[:, 1:-1, 1:-1, :-2]]
  transfers between devices with their start and end apart: 12 -> 0, of which waited for: 3 -> 0; matrix products, arithmetic and copies ran while one was open for 9% -> 0% of each run, Pallas kernels for 0% -> 0%
where the time goes in v1:
time: 55.3 us; the launch traced here: 55.1 us
  Pallas kernels  49.7 us (90%)
  local copies, waits for them, and re-layouts  4.18 us (8%)
  between operations  1.29 us (2%)
    pallas_call x1, Pallas kernels, shards(): pl.pallas_call(functools.partial(kernel, n_east, n_north), out_shape=(jax...  49.7 us
    unnamed x4, local copies, waits for them, and re-layouts  4.18 us

profile of v1, /device:TPU:1, one launch (start us, length us, event | category | flops | bytes accessed | tf_op | source)
XLA Modules:
  0.0 55.1 jit_solution(3575529842764307998)
XLA Ops:
  1.3 49.7 %shard_map.104 = (f32[5,16,32,256]{3,2,1,0:T(8,128)}, f32[4,8,12]{2,1,0:T(8,128)}) custom-call(f32[5,16,32,256]{3,2,1,0:T(8,128)} %start.1, f32[5,16,32,256]{3,2,1,0:T(8,128)} %source.1, f32[3,16,32,256]{3,2,1,0:T(8,128)} %base.1, f32[16,32,256]{2,1,0:T(8,128)} %eddy.1, s32[1,1]{1,0:T(1,128)S(6)} %copy.13.count, s32[1,1,1024]{2,1,0:T(1,128)} %cell.1, ...), custom_call_target="tpu_custom_call" | custom-call | tf_op jit(solution)/shard_map/pallas_call | solution.py:413
  51.0 0.0 copy-start
  51.0 3.6 %copy.14 = f32[5,16,32,256]{3,2,1,0:T(8,128)} copy(f32[5,16,32,256]{3,2,1,0:T(8,128)} %get-tuple-element.4) | data formatting | bytes 5242880
  54.5 0.0 copy-done
  54.5 0.6 %copy.15 = f32[4,8,12]{2,1,0:T(8,128)} copy(f32[4,8,12]{2,1,0:T(8,128)S(1)} %copy-done) | data formatting | bytes 3072
Async XLA Ops:
  51.0 3.6 %copy-start = (f32[4,8,12]{2,1,0:T(8,128)S(1)}, f32[4,8,12]{2,1,0:T(8,128)}, u32[]{:S(2)}) copy-start(f32[4,8,12]{2,1,0:T(8,128)} %get-tuple-element.5) | copy-start | bytes 4612

commit v2 on v1

v2 whole, which is shorter than its diff:
```python
import functools

import jax
import jax.numpy as jnp
from jax import lax
from jax.experimental import pallas as pl
from jax.experimental.pallas import tpu as pltpu
from jax.sharding import PartitionSpec as P

SECT = 8
TURB_DEV = 12
PITCH = 16
PAD = 8
MESH = pl.DeviceIdType.MESH
F32, BF16, I32 = jnp.float32, jnp.bfloat16, jnp.int32

VQ, EDDY, BASE = 0, 1, 2
EAST_UP, EAST_DOWN, NORTH_UP, NORTH_DOWN = 0, 1, 2, 3


def split(x):
    high = x.astype(BF16)
    return high, (x - high.astype(F32)).astype(BF16)


def kernel(
    n_east,
    n_north,
    start,
    source,
    base,
    eddy,
    count,
    cell_in,
    turbine_in,
    sector_in,
    weight_in,
    final,
    grad,
    v0,
    v1,
    flow,
    visc,
    src,
    coef,
    rest,
    curve,
    levels,
    found_acc,
    cell,
    turbine,
    sector,
    weight,
    parts,
    gathered,
    middle,
    totals,
    load_sem,
    send_sem,
    recv_sem,
    part_send,
    part_recv,
    total_send,
    total_recv,
):
    _, ce, cn, cz = start.shape
    slots = cell.shape[-1]
    east, north = lax.axis_index("east"), lax.axis_index("north")
    rows, planes = pl.ds(PAD, cn), pl.ds(1, ce)
    y, low_z, x = north // 8, (north // 4) % 2, north % 4
    n_plane, n_line = n_north // 2, n_east * 2
    in_plane, in_line = y * 4 + x, east * 2 + low_z

    def plane_peer(k):
        to = lax.rem(in_plane + k, n_plane)
        return to, {"north": (to // 4) * 8 + low_z * 4 + to % 4}

    def line_peer(k):
        to = lax.rem(in_line + k, n_line)
        return to, {"east": to // 2, "north": y * 8 + (to % 2) * 4 + x}

    loads = [
        pltpu.make_async_copy(eddy, visc, load_sem.at[0]),
        pltpu.make_async_copy(base, flow.at[:, planes, rows, :], load_sem.at[1]),
        pltpu.make_async_copy(cell_in, cell, load_sem.at[2]),
        pltpu.make_async_copy(weight_in, weight, load_sem.at[3]),
        pltpu.make_async_copy(start.at[0:4], v0.at[0:4, planes, rows, :], load_sem.at[4]),
        pltpu.make_async_copy(source, src, load_sem.at[5]),
        pltpu.make_async_copy(start.at[4:5], v0.at[4:5, planes, rows, :], load_sem.at[6]),
        pltpu.make_async_copy(turbine_in, turbine, load_sem.at[7]),
        pltpu.make_async_copy(sector_in, sector, load_sem.at[8]),
    ]

    barrier = pltpu.get_barrier_semaphore()

    def greet(target):
        pl.semaphore_signal(barrier, inc=1, device_id=target, device_id_type=MESH)

    greet({"north": lax.rem(north + 1, n_north)})
    greet({"north": lax.rem(north + n_north - 1, n_north)})
    for k in sorted(range(1, n_line), key=lambda k: (k % 2, min(k, n_line - k))):
        greet(line_peer(k)[1])
    for k in range(1, n_plane):
        greet(plane_peer(k)[1])
    for load in loads:
        load.start()

    def clear(at_end, plane, row):
        @pl.when(at_end)
        def _():
            for ref in (v0, v1, flow):
                if row is None:
                    ref[:, plane, rows, :] = jnp.zeros((ref.shape[0], cn, cz), F32)
                else:
                    ref[:, planes, row : row + 1, :] = jnp.zeros((ref.shape[0], ce, 1, cz), F32)

    clear(east == 0, 0, None)
    clear(east == n_east - 1, ce + 1, None)
    clear(north == 0, None, PAD - 1)
    clear(north == n_north - 1, None, PAD + cn)

    def halo(sweep, group, sent, landing, fields, padded):
        first, last = (1, ce) if padded else (0, ce - 1)
        low, high = (PAD, PAD + cn - 1) if padded else (0, cn - 1)
        row_all = rows if padded else slice(None)
        plane_all = planes if padded else slice(None)
        ends = [
            (
                sent.at[fields, last, row_all, :],
                landing.at[fields, 0, rows, :],
                {"east": east + 1},
                east < n_east - 1,
                east > 0,
            ),
            (
                sent.at[fields, first, row_all, :],
                landing.at[fields, ce + 1, rows, :],
                {"east": east - 1},
                east > 0,
                east < n_east - 1,
            ),
            (
                sent.at[fields, plane_all, high : high + 1, :],
                landing.at[fields, planes, PAD - 1 : PAD, :],
                {"north": north + 1},
                north < n_north - 1,
                north > 0,
            ),
            (
                sent.at[fields, plane_all, low : low + 1, :],
                landing.at[fields, planes, PAD + cn : PAD + cn + 1, :],
                {"north": north - 1},
                north > 0,
                north < n_north - 1,
            ),
        ]
        return [
            (
                pltpu.make_async_remote_copy(
                    src_ref=a,
                    dst_ref=b,
                    send_sem=send_sem.at[sweep, group, side],
                    recv_sem=recv_sem.at[sweep, group, side],
                    device_id=target,
                    device_id_type=MESH,
                ),
                sends,
                gets,
            )
            for side, (a, b, target, sends, gets) in enumerate(ends)
        ]

    def begin(group):
        for copy, sends, _ in group:
            pl.when(sends)(copy.start)

    def landed(group):
        for copy, _, gets in group:
            pl.when(gets)(copy.wait_recv)

    def left(group):
        for copy, sends, _ in group:
            pl.when(sends)(copy.wait_send)

    first_vq = halo(0, VQ, start, v0, slice(0, 4), False)
    first_eddy = halo(0, EDDY, start, v0, slice(4, 5), False)
    first_base = halo(0, BASE, base, flow, slice(0, 3), False)
    second_vq = halo(1, VQ, v1, v1, slice(0, 4), True)
    second_eddy = halo(1, EDDY, v1, v1, slice(4, 5), True)

    pl.semaphore_wait(barrier, n_plane + n_line)
    begin(first_vq)

    lane = lax.broadcasted_iota(I32, (cn, cz), 1)
    top, bottom = lane == cz - 1, lane == 0

    def loop(begin_at, end_at, body):
        def step_body(e, carry):
            body(e)
            return carry

        lax.fori_loop(begin_at, end_at, step_body, 0)

    for load in loads[:4]:
        load.wait()

    def prepare(e):
        w = 1.0 + visc[e]
        r1 = 1.0 / (6.0 * w + 1.0)
        half = 0.5 * r1
        wr = w * r1
        for k in range(3):
            hu = half * flow[k, e + 1, rows, :]
            above, below = wr + hu, wr - hu
            if k == 2:
                above, below = jnp.where(top, 0.0, above), jnp.where(bottom, 0.0, below)
            coef[2 * k, e] = above
            coef[2 * k + 1, e] = below
        coef[6, e] = half
        r2 = 1.0 / (6.0 * w + 2.0)
        rest[0, e] = r2
        rest[1, e] = w * r2

    loop(0, ce, prepare)
    begin(first_eddy)
    begin(first_base)

    entry_cell = cell[0]
    row_of = lax.shift_right_logical(entry_cell, cz.bit_length() - 1)
    level_of = lax.bitwise_and(entry_cell, cz - 1)
    level_hot = jnp.where(lax.broadcasted_iota(I32, (cz, slots), 0) == level_of, 1.0, 0.0).astype(BF16)
    levels[0:cz] = level_hot
    levels[cz : 2 * cz] = level_hot

    def gather(field, first_row):
        block_rows = field.shape[0]
        both = jnp.concatenate(split(field), axis=1)
        found = jnp.dot(both, levels[...], preferred_element_type=F32)
        here = lax.broadcasted_iota(I32, (block_rows, slots), 0) == row_of - first_row
        return jnp.sum(jnp.where(here, found, 0.0).reshape(block_rows // 8, 8, slots), axis=0)

    step = 4

    def upstream_block(p, acc):
        field = flow[0, pl.ds(p * step + 1, step), rows, :].reshape(step * cn, cz)
        return acc + gather(field, p * step * cn)

    upstream = lax.fori_loop(0, ce // step, upstream_block, jnp.zeros((8, slots), F32))
    upstream = jnp.sum(upstream, axis=0, keepdims=True)
    live = lax.broadcasted_iota(I32, (1, slots), 1) < count[0, 0]
    factor = jnp.where(live, weight[0] * upstream * jnp.abs(upstream), 0.0)

    def shifted(x):
        return pltpu.roll(x, cz - 1, 1), pltpu.roll(x, 1, 1)

    def relax_vq(e, old, new, offset, where_rows):
        def beside(c):
            x = old[c, e + 1, rows, :]
            return (
                x,
                old[c, e + 2, rows, :],
                old[c, e, rows, :],
                old[c, e + 1, pl.ds(PAD + 1, cn), :],
                old[c, e + 1, pl.ds(PAD - 1, cn), :],
                *shifted(x),
            )

        _, qe, qw, qn, qs, qu, qd = beside(3)
        qu, qd = jnp.where(top, 0.0, qu), jnp.where(bottom, 0.0, qd)
        grads = (qe - qw, qn - qs, qu - qd)
        sum_q = qe + qw + qn + qs + qu + qd
        half = coef[6, e]
        r1 = half + half
        diverge = None
        for c in range(3):
            _, *near = beside(c)
            total = r1 * src[c, e] - half * grads[c]
            for k in range(6):
                total = total + coef[k, e] * near[k]
            new[c, e + offset, where_rows, :] = total
            above, below = near[2 * c], near[2 * c + 1]
            if c == 2:
                above, below = jnp.where(top, 0.0, above), jnp.where(bottom, 0.0, below)
            slope = above - below
            diverge = slope if diverge is None else diverge + slope
        new[3, e + offset, where_rows, :] = (src[3, e] + sum_q - 0.5 * diverge) * (1.0 / 7.0)

    def around(ref, c, e):
        x = ref[c, e + 1, rows, :]
        up, down = shifted(x)
        up, down = jnp.where(top, 0.0, up), jnp.where(bottom, 0.0, down)
        total = ref[c, e + 2, rows, :] + ref[c, e, rows, :]
        total = total + ref[c, e + 1, pl.ds(PAD + 1, cn), :] + ref[c, e + 1, pl.ds(PAD - 1, cn), :]
        return total + up + down, x

    def relax_eddy(e, old, new, offset, where_rows, first):
        sum_m, _ = around(old, 4, e)
        total = rest[0, e] * src[4, e] + rest[1, e] * sum_m
        for c in range(3):
            if first:
                sum_u, u = around(flow, c, e)
                bend = (0.25 * rest[0, e]) * (sum_u - 6.0 * u)
                curve[c, e] = bend
            else:
                bend = curve[c, e]
            total = total + old[c, e + 1, rows, :] * bend
        new[4, e + offset, where_rows, :] = total

    for load in loads[4:]:
        load.wait()
    landed(first_vq[2:])
    sweep_one = lambda e: relax_vq(e, v0, v1, 1, rows)
    loop(1, ce - 1, sweep_one)
    landed(first_vq[:2])
    sweep_one(0)
    sweep_one(ce - 1)
    begin(second_vq)

    landed(first_eddy)
    landed(first_base)
    eddy_one = lambda e: relax_eddy(e, v0, v1, 1, rows, True)
    eddy_one(0)
    eddy_one(ce - 1)
    begin(second_eddy[:2])
    loop(1, ce - 1, eddy_one)
    begin(second_eddy[2:])

    landed(second_vq[2:])
    sweep_two = lambda e: relax_vq(e, v1, final, 0, slice(None))
    loop(1, ce - 1, sweep_two)
    half_inside = (ce - 2) // 2

    def gather_inside(c):
        acc = jnp.zeros((8, slots), F32)
        for part in range(2):
            p = 1 + part * half_inside
            field = final[c, p : p + half_inside].reshape(half_inside * cn, cz)
            acc = acc + gather(field, p * cn)
        found_acc[c] = acc

    def gather_edges(c):
        return gather(final[c, 0], 0) + gather(final[c, ce - 1], (ce - 1) * cn)

    loop(0, 3, gather_inside)
    landed(second_vq[:2])
    sweep_two(0)
    sweep_two(ce - 1)
    landed(second_eddy[2:])
    eddy_two = lambda e: relax_eddy(e, v1, final, 0, slice(None), False)
    loop(1, ce - 1, eddy_two)
    gather_inside(4)
    landed(second_eddy[:2])
    eddy_two(0)
    eddy_two(ce - 1)

    values = [jnp.sum(found_acc[c] + gather_edges(c), axis=0, keepdims=True) * factor for c in (0, 1, 2, 4)]
    terms = jnp.concatenate(values + [jnp.zeros((4, slots), F32)], axis=0)
    turbine_of = turbine[0]
    owner_of = lax.shift_right_logical(turbine_of * 5462, 16)
    place_of = sector[0] * PITCH + turbine_of - owner_of * TURB_DEV
    block_of = lax.bitwise_and(owner_of, ~7) + 2 * lax.bitwise_and(owner_of, 3)
    block_of = block_of + lax.bitwise_and(lax.shift_right_logical(owner_of, 2), 1)
    place_hot = jnp.where(lax.broadcasted_iota(I32, (SECT * PITCH, slots), 0) == place_of, 1.0, 0.0).astype(BF16)
    block_iota = lax.broadcasted_iota(I32, (n_north, 8, slots), 0)
    spread = jnp.where(block_iota == block_of[None], terms[None], 0.0).reshape(n_north * 8, slots)
    high, low = split(spread)
    contract = (((1,), (1,)), ((), ()))
    summed = lax.dot_general(high, place_hot, contract, preferred_element_type=F32)
    summed = summed + lax.dot_general(low, place_hot, contract, preferred_element_type=F32)
    parts[...] = summed.reshape(n_plane, 2, 8, SECT * PITCH)

    part_copies, total_copies = [], []
    for k in range(1, n_plane):
        to, target = plane_peer(k)
        part_copies.append(
            pltpu.make_async_remote_copy(
                src_ref=parts.at[to],
                dst_ref=gathered.at[in_plane],
                send_sem=part_send.at[k],
                recv_sem=part_recv.at[k],
                device_id=target,
                device_id_type=MESH,
            )
        )
    for k in range(1, n_line):
        to, target = line_peer(k)
        total_copies.append(
            pltpu.make_async_remote_copy(
                src_ref=middle.at[to % 2],
                dst_ref=totals.at[in_line],
                send_sem=total_send.at[k],
                recv_sem=total_recv.at[k],
                device_id=target,
                device_id_type=MESH,
            )
        )
    for copy in part_copies:
        copy.start()
    gathered[in_plane] = parts[in_plane]
    for copy in part_copies:
        copy.wait_recv()
    middle[...] = jnp.sum(gathered[...], axis=0)
    for copy in total_copies:
        copy.start()
    totals[in_line] = middle[low_z]
    for copy in total_copies:
        copy.wait_recv()
    whole = jnp.sum(totals[...], axis=0)
    for s in range(SECT):
        cut = whole[:, s * PITCH : s * PITCH + TURB_DEV]
        for c in range(4):
            grad[c, s : s + 1, :] = cut[c : c + 1]

    for copy in part_copies + total_copies:
        copy.wait_send()
    for group in (first_vq, first_base, first_eddy, second_vq, second_eddy):
        left(group)


def shards(n_east, n_north, *arrays):
    start, source, base, eddy, count, cell = arrays[:6]
    _, ce, cn, cz = start.shape
    slots = cell.shape[-1]
    padded = (ce + 2, cn + 2 * PAD, cz)
    n_plane, n_line = n_north // 2, n_east * 2
    hbm, vmem = pl.BlockSpec(memory_space=pltpu.HBM), pl.BlockSpec(memory_space=pltpu.VMEM)
    return tuple(
        pl.pallas_call(
            functools.partial(kernel, n_east, n_north),
            out_shape=(pltpu.VMEM(start.shape, F32), pltpu.VMEM((4, SECT, TURB_DEV), F32)),
            in_specs=[hbm] * 4 + [pl.BlockSpec(memory_space=pltpu.SMEM)] + [hbm] * 4,
            out_specs=(vmem, vmem),
            scratch_shapes=[
                pltpu.VMEM((5, *padded), F32),
                pltpu.VMEM((5, *padded), F32),
                pltpu.VMEM((3, *padded), F32),
                pltpu.VMEM((ce, cn, cz), F32),
                pltpu.VMEM((5, ce, cn, cz), F32),
                pltpu.VMEM((7, ce, cn, cz), F32),
                pltpu.VMEM((2, ce, cn, cz), F32),
                pltpu.VMEM((3, ce, cn, cz), F32),
                pltpu.VMEM((2 * cz, slots), BF16),
                pltpu.VMEM((5, 8, slots), F32),
                pltpu.VMEM((1, 1, slots), I32),
                pltpu.VMEM((1, 1, slots), I32),
                pltpu.VMEM((1, 1, slots), I32),
                pltpu.VMEM((1, 1, slots), F32),
                pltpu.VMEM((n_plane, 2, 8, SECT * PITCH), F32),
                pltpu.VMEM((n_plane, 2, 8, SECT * PITCH), F32),
                pltpu.VMEM((2, 8, SECT * PITCH), F32),
                pltpu.VMEM((n_line, 8, SECT * PITCH), F32),
                pltpu.SemaphoreType.DMA((9,)),
                pltpu.SemaphoreType.DMA((2, 3, 4)),
                pltpu.SemaphoreType.DMA((2, 3, 4)),
                pltpu.SemaphoreType.DMA((n_plane,)),
                pltpu.SemaphoreType.DMA((n_plane,)),
                pltpu.SemaphoreType.DMA((n_line,)),
                pltpu.SemaphoreType.DMA((n_line,)),
            ],
            compiler_params=pltpu.CompilerParams(
                collective_id=0, has_side_effects=True, vmem_limit_bytes=40 * 1024 * 1024
            ),
        )(*(pltpu.with_memory_space_constraint(x, pltpu.HBM) if x.dtype == F32 or x.ndim > 2 else x for x in arrays))
    )


def solution(mesh):
    fields, scalars = P(None, "east", "north", None), P("east", "north", None)
    return jax.shard_map(
        functools.partial(shards, mesh.shape["east"], mesh.shape["north"]),
        mesh=mesh,
        in_specs=(fields, fields, fields, scalars, P("east", "north"), scalars, scalars, scalars, scalars),
        out_specs=(fields, P(None, None, "north")),
        check_vma=False,
    )
```

time: 55.3 us -> 50.8 us (0.919)
  Pallas kernels: 49.7 us -> 47.3 us
  local copies, waits for them, and re-layouts: 4.18 us -> 2.1 us
    pallas_call x1, Pallas kernels: 49.7 us -> 47.3 us  [shards(): pl.pallas_call(functools.partial(kernel, n_east, n_north), out_shape=(plt...]
    unnamed x4 -> x2, local copies, waits for them, and re-layouts: 4.18 us -> 2.1 us
where the time goes in v2:
time: 50.8 us; the launch traced here: 50.7 us
  Pallas kernels  47.3 us (93%)
  local copies, waits for them, and re-layouts  2.1 us (4%)
  between operations  1.29 us (3%)
    pallas_call x1, Pallas kernels, shards(): pl.pallas_call(functools.partial(kernel, n_east, n_north), out_shape=(plt...  47.3 us
    unnamed x2, local copies, waits for them, and re-layouts  2.1 us

profile of v2, /device:TPU:1, one launch (start us, length us, event | category | flops | bytes accessed | tf_op | source)
XLA Modules:
  0.0 50.7 jit_solution(5392538684515491851)
XLA Ops:
  1.3 47.3 %shard_map.104 = (f32[5,16,32,256]{3,2,1,0:T(8,128)S(1)}, f32[4,8,12]{2,1,0:T(8,128)S(1)}) custom-call(f32[5,16,32,256]{3,2,1,0:T(8,128)} %start.1, f32[5,16,32,256]{3,2,1,0:T(8,128)} %source.1, f32[3,16,32,256]{3,2,1,0:T(8,128)} %base.1, f32[16,32,256]{2,1,0:T(8,128)} %eddy.1, s32[1,1]{1,0:T(1,128)S(6)} %copy.15.count, s32[1,1,1024]{2,1,0:T(1,128)} %cell_in.1, ...), custom_call_target="tpu_custom_call" | custom-call | tf_op jit(solution)/shard_map/pallas_call | solution.py:428
  48.6 1.5 %copy.13 = f32[5,16,32,256]{3,2,1,0:T(8,128)} copy(f32[5,16,32,256]{3,2,1,0:T(8,128)S(1)} %get-tuple-element.2) | data formatting | bytes 5242880
  50.1 0.6 %copy.14 = f32[4,8,12]{2,1,0:T(8,128)} copy(f32[4,8,12]{2,1,0:T(8,128)S(1)} %get-tuple-element.3) | data formatting | bytes 3072

commit v3 on v2

--- a/solution.py
+++ b/solution.py
@@ -47,6 +47,8 @@
     curve,
     levels,
     found_acc,
+    beside_first,
+    beside_second,
     cell,
     turbine,
     sector,
@@ -105,21 +107,30 @@
     for load in loads:
         load.start()
 
-    def clear(at_end, plane, row):
+    for ref in (v0, v1, flow):
+        for row in (PAD - 1, PAD + cn):
+            ref[:, planes, row : row + 1, :] = jnp.zeros((ref.shape[0], ce, 1, cz), F32)
+    for ref in (beside_first, beside_second):
+        ref[:, :, 1:15, :] = jnp.zeros((ref.shape[0], ce, 14, cz), F32)
+
+    def clear_plane(at_end, plane):
         @pl.when(at_end)
         def _():
             for ref in (v0, v1, flow):
-                if row is None:
-                    ref[:, plane, rows, :] = jnp.zeros((ref.shape[0], cn, cz), F32)
-                else:
-                    ref[:, planes, row : row + 1, :] = jnp.zeros((ref.shape[0], ce, 1, cz), F32)
-
-    clear(east == 0, 0, None)
-    clear(east == n_east - 1, ce + 1, None)
-    clear(north == 0, None, PAD - 1)
-    clear(north == n_north - 1, None, PAD + cn)
-
-    def halo(sweep, group, sent, landing, fields, padded):
+                ref[:, plane, rows, :] = jnp.zeros((ref.shape[0], cn, cz), F32)
+
+    def clear_row(at_end, row):
+        @pl.when(at_end)
+        def _():
+            for ref in (beside_first, beside_second):
+                ref[:, :, row : row + 1, :] = jnp.zeros((ref.shape[0], ce, 1, cz), F32)
+
+    clear_plane(east == 0, 0)
+    clear_plane(east == n_east - 1, ce + 1)
+    clear_row(north == 0, 0)
+    clear_row(north == n_north - 1, 15)
+
+    def halo(sweep, group, sent, landing, fields, padded, row_landing, row_fields):
         first, last = (1, ce) if padded else (0, ce - 1)
         low, high = (PAD, PAD + cn - 1) if padded else (0, cn - 1)
         row_all = rows if padded else slice(None)
@@ -141,14 +152,14 @@
             ),
             (
                 sent.at[fields, plane_all, high : high + 1, :],
-                landing.at[fields, planes, PAD - 1 : PAD, :],
+                row_landing.at[row_fields, :, 0:1, :],
                 {"north": north + 1},
                 north < n_north - 1,
                 north > 0,
             ),
             (
                 sent.at[fields, plane_all, low : low + 1, :],
-                landing.at[fields, planes, PAD + cn : PAD + cn + 1, :],
+                row_landing.at[row_fields, :, 15:16, :],
                 {"north": north - 1},
                 north > 0,
                 north < n_north - 1,
@@ -182,11 +193,11 @@
         for copy, sends, _ in group:
             pl.when(sends)(copy.wait_send)
 
-    first_vq = halo(0, VQ, start, v0, slice(0, 4), False)
-    first_eddy = halo(0, EDDY, start, v0, slice(4, 5), False)
-    first_base = halo(0, BASE, base, flow, slice(0, 3), False)
-    second_vq = halo(1, VQ, v1, v1, slice(0, 4), True)
-    second_eddy = halo(1, EDDY, v1, v1, slice(4, 5), True)
+    first_vq = halo(0, VQ, start, v0, slice(0, 4), False, beside_first, slice(0, 4))
+    first_eddy = halo(0, EDDY, start, v0, slice(4, 5), False, beside_first, slice(4, 5))
+    first_base = halo(0, BASE, base, flow, slice(0, 3), False, beside_first, slice(5, 8))
+    second_vq = halo(1, VQ, v1, v1, slice(0, 4), True, beside_second, slice(0, 4))
+    second_eddy = halo(1, EDDY, v1, v1, slice(4, 5), True, beside_second, slice(4, 5))
 
     pl.semaphore_wait(barrier, n_plane + n_line)
     begin(first_vq)
@@ -232,18 +243,23 @@
     levels[0:cz] = level_hot
     levels[cz : 2 * cz] = level_hot
 
-    def gather(field, first_row):
-        block_rows = field.shape[0]
+    def gather(field, row_ids, comps):
+        block_rows = field.shape[0] // comps
         both = jnp.concatenate(split(field), axis=1)
         found = jnp.dot(both, levels[...], preferred_element_type=F32)
-        here = lax.broadcasted_iota(I32, (block_rows, slots), 0) == row_of - first_row
-        return jnp.sum(jnp.where(here, found, 0.0).reshape(block_rows // 8, 8, slots), axis=0)
+        here = row_ids == row_of
+        sums = []
+        for c in range(comps):
+            kept = jnp.where(here, found[c * block_rows : (c + 1) * block_rows], 0.0)
+            sums.append(jnp.sum(kept.reshape(block_rows // 8, 8, slots), axis=0))
+        return sums
 
     step = 4
 
     def upstream_block(p, acc):
         field = flow[0, pl.ds(p * step + 1, step), rows, :].reshape(step * cn, cz)
-        return acc + gather(field, p * step * cn)
+        row_ids = lax.broadcasted_iota(I32, (step * cn, slots), 0) + p * step * cn
+        return acc + gather(field, row_ids, 1)[0]
 
     upstream = lax.fori_loop(0, ce // step, upstream_block, jnp.zeros((8, slots), F32))
     upstream = jnp.sum(upstream, axis=0, keepdims=True)
@@ -306,54 +322,94 @@
             total = total + old[c, e + 1, rows, :] * bend
         new[4, e + offset, where_rows, :] = total
 
+    def sides():
+        return ((0, 0, 3, 1.0), (cn - 8, 8, 2, -1.0))
+
+    def fix_vq(e, landing, new, offset, pad):
+        for row, tile, k, sign in sides():
+            near = [landing[c, e, tile : tile + 8, :] for c in range(4)]
+            here = slice(row, row + 8)
+            for c in range(3):
+                add = coef[k, e, here, :] * near[c]
+                if c == 1:
+                    add = add + (sign * coef[6, e, here, :]) * near[3]
+                new[c, e + offset, pad + row : pad + row + 8, :] += add
+            new[3, e + offset, pad + row : pad + row + 8, :] += (near[3] + (0.5 * sign) * near[1]) * (1.0 / 7.0)
+
+    def fix_eddy(e, landing, old, new, offset, pad, first):
+        for row, tile, _, _ in sides():
+            here = slice(row, row + 8)
+            add = rest[1, e, here, :] * landing[4, e, tile : tile + 8, :]
+            if first:
+                quarter = 0.25 * rest[0, e, here, :]
+                for c in range(3):
+                    bend = quarter * landing[5 + c, e, tile : tile + 8, :]
+                    curve[c, e, here, :] += bend
+                    add = add + old[c, e + 1, PAD + row : PAD + row + 8, :] * bend
+            new[4, e + offset, pad + row : pad + row + 8, :] += add
+
     for load in loads[4:]:
         load.wait()
-    landed(first_vq[2:])
-    sweep_one = lambda e: relax_vq(e, v0, v1, 1, rows)
-    loop(1, ce - 1, sweep_one)
-    landed(first_vq[:2])
-    sweep_one(0)
-    sweep_one(ce - 1)
+    vq_one = lambda e: relax_vq(e, v0, v1, 1, rows)
+    eddy_one = lambda e: relax_eddy(e, v0, v1, 1, rows, True)
+    loop(1, ce - 1, vq_one)
+    loop(1, ce - 1, eddy_one)
+    landed(first_vq)
+    vq_one(0)
+    vq_one(ce - 1)
+    loop(0, ce, lambda e: fix_vq(e, beside_first, v1, 1, PAD))
     begin(second_vq)
-
     landed(first_eddy)
     landed(first_base)
-    eddy_one = lambda e: relax_eddy(e, v0, v1, 1, rows, True)
     eddy_one(0)
     eddy_one(ce - 1)
-    begin(second_eddy[:2])
-    loop(1, ce - 1, eddy_one)
-    begin(second_eddy[2:])
-
-    landed(second_vq[2:])
-    sweep_two = lambda e: relax_vq(e, v1, final, 0, slice(None))
-    loop(1, ce - 1, sweep_two)
+    loop(0, ce, lambda e: fix_eddy(e, beside_first, v0, v1, 1, PAD, True))
+    begin(second_eddy)
+
+    vq_two = lambda e: relax_vq(e, v1, final, 0, slice(None))
+    eddy_two = lambda e: relax_eddy(e, v1, final, 0, slice(None), False)
+    loop(1, ce - 1, vq_two)
+    loop(1, ce - 1, eddy_two)
     half_inside = (ce - 2) // 2
+
+    def inner_ids(count_rows, first_row):
+        ids = lax.broadcasted_iota(I32, (count_rows, slots), 0)
+        in_plane_row = lax.rem(ids, cn)
+        return jnp.where((in_plane_row == 0) | (in_plane_row == cn - 1), -1, ids + first_row)
 
     def gather_inside(c):
         acc = jnp.zeros((8, slots), F32)
         for part in range(2):
             p = 1 + part * half_inside
             field = final[c, p : p + half_inside].reshape(half_inside * cn, cz)
-            acc = acc + gather(field, p * cn)
+            acc = acc + gather(field, inner_ids(half_inside * cn, p * cn), 1)[0]
         found_acc[c] = acc
 
-    def gather_edges(c):
-        return gather(final[c, 0], 0) + gather(final[c, ce - 1], (ce - 1) * cn)
-
     loop(0, 3, gather_inside)
-    landed(second_vq[:2])
-    sweep_two(0)
-    sweep_two(ce - 1)
-    landed(second_eddy[2:])
-    eddy_two = lambda e: relax_eddy(e, v1, final, 0, slice(None), False)
-    loop(1, ce - 1, eddy_two)
     gather_inside(4)
-    landed(second_eddy[:2])
+    landed(second_vq)
+    vq_two(0)
+    vq_two(ce - 1)
+    loop(0, ce, lambda e: fix_vq(e, beside_second, final, 0, 0))
+    landed(second_eddy)
     eddy_two(0)
     eddy_two(ce - 1)
-
-    values = [jnp.sum(found_acc[c] + gather_edges(c), axis=0, keepdims=True) * factor for c in (0, 1, 2, 4)]
+    loop(0, ce, lambda e: fix_eddy(e, beside_second, v1, final, 0, 0, False))
+
+    edge_fields = []
+    for c in (0, 1, 2, 4):
+        for plane in (0, ce - 1):
+            edge_fields.append(final[c, plane])
+        for row in (0, cn - 1):
+            edge_fields.append(final[c, :, row, :])
+    plane_iota = lax.broadcasted_iota(I32, (ce, slots), 0) * cn
+    edge_ids = jnp.concatenate(
+        [inner_ids(cn, 0), inner_ids(cn, (ce - 1) * cn), plane_iota, plane_iota + cn - 1], axis=0
+    )
+    edge_sums = gather(jnp.concatenate(edge_fields, axis=0), edge_ids, 4)
+    values = [
+        jnp.sum(found_acc[c] + edge, axis=0, keepdims=True) * factor for c, edge in zip((0, 1, 2, 4), edge_sums)
+    ]
     terms = jnp.concatenate(values + [jnp.zeros((4, slots), F32)], axis=0)
     turbine_of = turbine[0]
     owner_of = lax.shift_right_logical(turbine_of * 5462, 16)
@@ -441,6 +497,8 @@
                 pltpu.VMEM((3, ce, cn, cz), F32),
                 pltpu.VMEM((2 * cz, slots), BF16),
                 pltpu.VMEM((5, 8, slots), F32),
+                pltpu.VMEM((8, ce, 16, cz), F32),
+                pltpu.VMEM((5, ce, 16, cz), F32),
                 pltpu.VMEM((1, 1, slots), I32),
                 pltpu.VMEM((1, 1, slots), I32),
                 pltpu.VMEM((1, 1, slots), I32),

time: 50.8 us -> 46.7 us (0.919)
  Pallas kernels: 47.3 us -> 43.3 us
    pallas_call x1, Pallas kernels: 47.3 us -> 43.3 us  [shards(): pl.pallas_call(functools.partial(kernel, n_east, n_north), out_shape=(plt...]
where the time goes in v3:
time: 46.7 us; the launch traced here: 46.6 us
  Pallas kernels  43.3 us (93%)
  local copies, waits for them, and re-layouts  2.1 us (4%)
  between operations  1.29 us (3%)
    pallas_call x1, Pallas kernels, shards(): pl.pallas_call(functools.partial(kernel, n_east, n_north), out_shape=(plt...  43.3 us
    unnamed x2, local copies, waits for them, and re-layouts  2.1 us

profile of v3, /device:TPU:1, one launch (start us, length us, event | category | flops | bytes accessed | tf_op | source)
XLA Modules:
  0.0 46.6 jit_solution(10255673005616795355)
XLA Ops:
  1.3 43.3 %shard_map.104 = (f32[5,16,32,256]{3,2,1,0:T(8,128)S(1)}, f32[4,8,12]{2,1,0:T(8,128)S(1)}) custom-call(f32[5,16,32,256]{3,2,1,0:T(8,128)} %start.1, f32[5,16,32,256]{3,2,1,0:T(8,128)} %source.1, f32[3,16,32,256]{3,2,1,0:T(8,128)} %base.1, f32[16,32,256]{2,1,0:T(8,128)} %eddy.1, s32[1,1]{1,0:T(1,128)S(6)} %copy.15.count, s32[1,1,1024]{2,1,0:T(1,128)} %cell_in.1, ...), custom_call_target="tpu_custom_call" | custom-call | tf_op jit(solution)/shard_map/pallas_call | solution.py:484
  44.5 1.5 %copy.13 = f32[5,16,32,256]{3,2,1,0:T(8,128)} copy(f32[5,16,32,256]{3,2,1,0:T(8,128)S(1)} %get-tuple-element.2) | data formatting | bytes 5242880
  46.0 0.6 %copy.14 = f32[4,8,12]{2,1,0:T(8,128)} copy(f32[4,8,12]{2,1,0:T(8,128)S(1)} %get-tuple-element.3) | data formatting | bytes 3072

commit v4 on v3

--- a/solution.py
+++ b/solution.py
@@ -47,6 +47,8 @@
     curve,
     levels,
     found_acc,
+    places,
+    blocks,
     beside_first,
     beside_second,
     cell,
@@ -266,6 +268,17 @@
     live = lax.broadcasted_iota(I32, (1, slots), 1) < count[0, 0]
     factor = jnp.where(live, weight[0] * upstream * jnp.abs(upstream), 0.0)
 
+    for load in loads[7:]:
+        load.wait()
+    turbine_of = turbine[0]
+    owner_of = lax.shift_right_logical(turbine_of * 5462, 16)
+    place_of = sector[0] * PITCH + turbine_of - owner_of * TURB_DEV
+    block_of = lax.bitwise_and(owner_of, ~7) + 2 * lax.bitwise_and(owner_of, 3)
+    block_of = block_of + lax.bitwise_and(lax.shift_right_logical(owner_of, 2), 1)
+    places[...] = jnp.where(lax.broadcasted_iota(I32, places.shape, 0) == place_of, 1.0, 0.0).astype(BF16)
+    block_iota = lax.shift_right_logical(lax.broadcasted_iota(I32, blocks.shape, 0), 4)
+    blocks[...] = jnp.where(block_iota == block_of, 1.0, 0.0).astype(BF16)
+
     def shifted(x):
         return pltpu.roll(x, cz - 1, 1), pltpu.roll(x, 1, 1)
 
@@ -348,7 +361,7 @@
                     add = add + old[c, e + 1, PAD + row : PAD + row + 8, :] * bend
             new[4, e + offset, pad + row : pad + row + 8, :] += add
 
-    for load in loads[4:]:
+    for load in loads[4:7]:
         load.wait()
     vq_one = lambda e: relax_vq(e, v0, v1, 1, rows)
     eddy_one = lambda e: relax_eddy(e, v0, v1, 1, rows, True)
@@ -359,16 +372,19 @@
     vq_one(ce - 1)
     loop(0, ce, lambda e: fix_vq(e, beside_first, v1, 1, PAD))
     begin(second_vq)
+    vq_two = lambda e: relax_vq(e, v1, final, 0, slice(None))
+    loop(1, ce - 1, vq_two)
     landed(first_eddy)
     landed(first_base)
-    eddy_one(0)
-    eddy_one(ce - 1)
-    loop(0, ce, lambda e: fix_eddy(e, beside_first, v0, v1, 1, PAD, True))
-    begin(second_eddy)
-
-    vq_two = lambda e: relax_vq(e, v1, final, 0, slice(None))
+    fix_eddy_one = lambda e: fix_eddy(e, beside_first, v0, v1, 1, PAD, True)
+    for e in (0, ce - 1):
+        eddy_one(e)
+        fix_eddy_one(e)
+    begin(second_eddy[:2])
+    loop(1, ce - 1, fix_eddy_one)
+    begin(second_eddy[2:])
+
     eddy_two = lambda e: relax_eddy(e, v1, final, 0, slice(None), False)
-    loop(1, ce - 1, vq_two)
     loop(1, ce - 1, eddy_two)
     half_inside = (ce - 2) // 2
 
@@ -411,18 +427,11 @@
         jnp.sum(found_acc[c] + edge, axis=0, keepdims=True) * factor for c, edge in zip((0, 1, 2, 4), edge_sums)
     ]
     terms = jnp.concatenate(values + [jnp.zeros((4, slots), F32)], axis=0)
-    turbine_of = turbine[0]
-    owner_of = lax.shift_right_logical(turbine_of * 5462, 16)
-    place_of = sector[0] * PITCH + turbine_of - owner_of * TURB_DEV
-    block_of = lax.bitwise_and(owner_of, ~7) + 2 * lax.bitwise_and(owner_of, 3)
-    block_of = block_of + lax.bitwise_and(lax.shift_right_logical(owner_of, 2), 1)
-    place_hot = jnp.where(lax.broadcasted_iota(I32, (SECT * PITCH, slots), 0) == place_of, 1.0, 0.0).astype(BF16)
-    block_iota = lax.broadcasted_iota(I32, (n_north, 8, slots), 0)
-    spread = jnp.where(block_iota == block_of[None], terms[None], 0.0).reshape(n_north * 8, slots)
-    high, low = split(spread)
+    both = jnp.concatenate(split(terms), axis=0)
+    spread = blocks[...] * jnp.concatenate([both] * n_north, axis=0)
     contract = (((1,), (1,)), ((), ()))
-    summed = lax.dot_general(high, place_hot, contract, preferred_element_type=F32)
-    summed = summed + lax.dot_general(low, place_hot, contract, preferred_element_type=F32)
+    summed = lax.dot_general(spread, places[...], contract, preferred_element_type=F32)
+    summed = jnp.sum(summed.reshape(n_north, 2, 8, SECT * PITCH), axis=1)
     parts[...] = summed.reshape(n_plane, 2, 8, SECT * PITCH)
 
     part_copies, total_copies = [], []
@@ -473,6 +482,15 @@
         left(group)
 
 
+def store(fields, sums, fields_out, sums_out, sem):
+    copies = [pltpu.make_async_copy(sums, sums_out, sem.at[0])]
+    copies += [pltpu.make_async_copy(fields.at[c], fields_out.at[c], sem.at[c + 1]) for c in range(fields.shape[0])]
+    for copy in copies:
+        copy.start()
+    for copy in copies:
+        copy.wait()
+
+
 def shards(n_east, n_north, *arrays):
     start, source, base, eddy, count, cell = arrays[:6]
     _, ce, cn, cz = start.shape
@@ -480,7 +498,7 @@
     padded = (ce + 2, cn + 2 * PAD, cz)
     n_plane, n_line = n_north // 2, n_east * 2
     hbm, vmem = pl.BlockSpec(memory_space=pltpu.HBM), pl.BlockSpec(memory_space=pltpu.VMEM)
-    return tuple(
+    in_vmem = (
         pl.pallas_call(
             functools.partial(kernel, n_east, n_north),
             out_shape=(pltpu.VMEM(start.shape, F32), pltpu.VMEM((4, SECT, TURB_DEV), F32)),
@@ -497,6 +515,8 @@
                 pltpu.VMEM((3, ce, cn, cz), F32),
                 pltpu.VMEM((2 * cz, slots), BF16),
                 pltpu.VMEM((5, 8, slots), F32),
+                pltpu.VMEM((SECT * PITCH, slots), BF16),
+                pltpu.VMEM((n_north * 16, slots), BF16),
                 pltpu.VMEM((8, ce, 16, cz), F32),
                 pltpu.VMEM((5, ce, 16, cz), F32),
                 pltpu.VMEM((1, 1, slots), I32),
@@ -520,6 +540,17 @@
             ),
         )(*(pltpu.with_memory_space_constraint(x, pltpu.HBM) if x.dtype == F32 or x.ndim > 2 else x for x in arrays))
     )
+    parts = start.shape[0]
+    return tuple(
+        pl.pallas_call(
+            store,
+            out_shape=tuple(jax.ShapeDtypeStruct(x.shape, x.dtype) for x in in_vmem),
+            in_specs=[vmem] * 2,
+            out_specs=(hbm, hbm),
+            scratch_shapes=[pltpu.SemaphoreType.DMA((parts + 1,))],
+            compiler_params=pltpu.CompilerParams(vmem_limit_bytes=8 * 1024 * 1024),
+        )(*(pltpu.with_memory_space_constraint(x, pltpu.VMEM) for x in in_vmem))
+    )
 
 
 def solution(mesh):

time: 46.7 us -> 43.2 us (0.925)
  local copies, waits for them, and re-layouts: 2.1 us -> 0 us
  Pallas kernels: 43.3 us -> 41.9 us
    pallas_call x1, Pallas kernels: 43.3 us -> 40.3 us  [shards(): pl.pallas_call(functools.partial(kernel, n_east, n_north), out_shape=(plt...]
    unnamed x2 -> x0, local copies, waits for them, and re-layouts: 2.1 us -> none
    pallas_call x0 -> x1, Pallas kernels: none -> 1.54 us  [shards(): pl.pallas_call(store, out_shape=tuple((jax.ShapeDtypeStruct(x.shape, x.dt...]
where the time goes in v4:
time: 43.2 us; the launch traced here: 43.1 us
  Pallas kernels  41.9 us (97%)
  between operations  1.29 us (3%)
    pallas_call x1, Pallas kernels, shards(): pl.pallas_call(functools.partial(kernel, n_east, n_north), out_shape=(plt...  40.3 us
    pallas_call x1, Pallas kernels, shards(): pl.pallas_call(store, out_shape=tuple((jax.ShapeDtypeStruct(x.shape, x.dt...  1.54 us

profile of v4, /device:TPU:1, one launch (start us, length us, event | category | flops | bytes accessed | tf_op | source)
XLA Modules:
  0.0 43.1 jit_solution(15656477964543475968)
XLA Ops:
  1.3 40.3 %shard_map.104 = (f32[5,16,32,256]{3,2,1,0:T(8,128)S(1)}, f32[4,8,12]{2,1,0:T(8,128)S(1)}) custom-call(f32[5,16,32,256]{3,2,1,0:T(8,128)} %start.1, f32[5,16,32,256]{3,2,1,0:T(8,128)} %source.1, f32[3,16,32,256]{3,2,1,0:T(8,128)} %base.1, f32[16,32,256]{2,1,0:T(8,128)} %eddy.1, s32[1,1]{1,0:T(1,128)S(6)} %copy.11.count, s32[1,1,1024]{2,1,0:T(1,128)} %cell_in.1, ...), custom_call_target="tpu_custom_call" | custom-call | tf_op jit(solution)/shard_map/pallas_call | solution.py:502
  41.6 1.5 %shard_map.105 = (f32[5,16,32,256]{3,2,1,0:T(8,128)}, f32[4,8,12]{2,1,0:T(8,128)}) custom-call(f32[5,16,32,256]{3,2,1,0:T(8,128)S(1)} %get-tuple-element.4.fields, f32[4,8,12]{2,1,0:T(8,128)S(1)} %get-tuple-element.5.sums), custom_call_target="tpu_custom_call" | custom-call | tf_op jit(solution)/shard_map/pallas_call | solution.py:545

commit v5 on v4

--- a/solution.py
+++ b/solution.py
@@ -75,13 +75,29 @@
     n_plane, n_line = n_north // 2, n_east * 2
     in_plane, in_line = y * 4 + x, east * 2 + low_z
 
+    n_y, n_z = n_plane // 4, n_east
+    z = east // 2 * 2 + low_z
+    core = east % 2
+
+    def hops(step, size):
+        return min(step, size - step)
+
+    plane_steps = [(dy, dx) for dy in range(n_y) for dx in range(4) if (dy, dx) != (0, 0)]
+    plane_steps.sort(key=lambda d: -hops(d[0], n_y) - hops(d[1], 4))
+    line_steps = [(dz, flip) for dz in range(n_z) for flip in range(2) if (dz, flip) != (0, 0)]
+    line_steps.sort(key=lambda d: -2 * hops(d[0], n_z) - d[1])
+
     def plane_peer(k):
-        to = lax.rem(in_plane + k, n_plane)
-        return to, {"north": (to // 4) * 8 + low_z * 4 + to % 4}
+        dy, dx = plane_steps[k - 1]
+        to_y, to_x = lax.rem(y + dy, n_y), lax.rem(x + dx, 4)
+        return to_y * 4 + to_x, {"north": to_y * 8 + low_z * 4 + to_x}
 
     def line_peer(k):
-        to = lax.rem(in_line + k, n_line)
-        return to, {"east": to // 2, "north": y * 8 + (to % 2) * 4 + x}
+        dz, flip = line_steps[k - 1]
+        to_z = lax.rem(z + dz, n_z)
+        to_core = 1 - core if flip else core
+        to_east, to_low = to_z // 2 * 2 + to_core, to_z % 2
+        return to_east * 2 + to_low, {"east": to_east, "north": y * 8 + to_low * 4 + x}
 
     loads = [
         pltpu.make_async_copy(eddy, visc, load_sem.at[0]),
@@ -102,7 +118,7 @@
 
     greet({"north": lax.rem(north + 1, n_north)})
     greet({"north": lax.rem(north + n_north - 1, n_north)})
-    for k in sorted(range(1, n_line), key=lambda k: (k % 2, min(k, n_line - k))):
+    for k in range(n_line - 1, 0, -1):
         greet(line_peer(k)[1])
     for k in range(1, n_plane):
         greet(plane_peer(k)[1])
@@ -207,12 +223,13 @@
     lane = lax.broadcasted_iota(I32, (cn, cz), 1)
     top, bottom = lane == cz - 1, lane == 0
 
-    def loop(begin_at, end_at, body):
-        def step_body(e, carry):
-            body(e)
+    def loop(begin_at, end_at, body, together=1):
+        def step_body(i, carry):
+            for j in range(together):
+                body(begin_at + i * together + j)
             return carry
 
-        lax.fori_loop(begin_at, end_at, step_body, 0)
+        lax.fori_loop(0, (end_at - begin_at) // together, step_body, 0)
 
     for load in loads[:4]:
         load.wait()
@@ -273,11 +290,12 @@
     turbine_of = turbine[0]
     owner_of = lax.shift_right_logical(turbine_of * 5462, 16)
     place_of = sector[0] * PITCH + turbine_of - owner_of * TURB_DEV
-    block_of = lax.bitwise_and(owner_of, ~7) + 2 * lax.bitwise_and(owner_of, 3)
-    block_of = block_of + lax.bitwise_and(lax.shift_right_logical(owner_of, 2), 1)
+    block_of = 4 * lax.shift_right_logical(owner_of, 3) + lax.bitwise_and(owner_of, 3)
+    part_of = 2 * block_of + lax.bitwise_and(lax.shift_right_logical(owner_of, 2), 1)
     places[...] = jnp.where(lax.broadcasted_iota(I32, places.shape, 0) == place_of, 1.0, 0.0).astype(BF16)
-    block_iota = lax.shift_right_logical(lax.broadcasted_iota(I32, blocks.shape, 0), 4)
-    blocks[...] = jnp.where(block_iota == block_of, 1.0, 0.0).astype(BF16)
+    row_iota = lax.broadcasted_iota(I32, blocks.shape, 0)
+    part_iota = 2 * lax.shift_right_logical(row_iota, 4) + lax.bitwise_and(lax.shift_right_logical(row_iota, 2), 1)
+    blocks[...] = jnp.where(part_iota == part_of, 1.0, 0.0).astype(BF16)
 
     def shifted(x):
         return pltpu.roll(x, cz - 1, 1), pltpu.roll(x, 1, 1)
@@ -370,10 +388,26 @@
     landed(first_vq)
     vq_one(0)
     vq_one(ce - 1)
-    loop(0, ce, lambda e: fix_vq(e, beside_first, v1, 1, PAD))
+    loop(0, ce, lambda e: fix_vq(e, beside_first, v1, 1, PAD), 4)
     begin(second_vq)
     vq_two = lambda e: relax_vq(e, v1, final, 0, slice(None))
     loop(1, ce - 1, vq_two)
+    half_inside = (ce - 2) // 2
+
+    def inner_ids(count_rows, first_row):
+        ids = lax.broadcasted_iota(I32, (count_rows, slots), 0)
+        in_plane_row = lax.rem(ids, cn)
+        return jnp.where((in_plane_row == 0) | (in_plane_row == cn - 1), -1, ids + first_row)
+
+    def gather_inside(c):
+        acc = jnp.zeros((8, slots), F32)
+        for part in range(2):
+            p = 1 + part * half_inside
+            field = final[c, p : p + half_inside].reshape(half_inside * cn, cz)
+            acc = acc + gather(field, inner_ids(half_inside * cn, p * cn), 1)[0]
+        found_acc[c] = acc
+
+    loop(0, 2, gather_inside)
     landed(first_eddy)
     landed(first_base)
     fix_eddy_one = lambda e: fix_eddy(e, beside_first, v0, v1, 1, PAD, True)
@@ -381,58 +415,45 @@
         eddy_one(e)
         fix_eddy_one(e)
     begin(second_eddy[:2])
-    loop(1, ce - 1, fix_eddy_one)
+    loop(1, ce - 1, fix_eddy_one, 2)
     begin(second_eddy[2:])
 
     eddy_two = lambda e: relax_eddy(e, v1, final, 0, slice(None), False)
     loop(1, ce - 1, eddy_two)
-    half_inside = (ce - 2) // 2
-
-    def inner_ids(count_rows, first_row):
-        ids = lax.broadcasted_iota(I32, (count_rows, slots), 0)
-        in_plane_row = lax.rem(ids, cn)
-        return jnp.where((in_plane_row == 0) | (in_plane_row == cn - 1), -1, ids + first_row)
-
-    def gather_inside(c):
-        acc = jnp.zeros((8, slots), F32)
-        for part in range(2):
-            p = 1 + part * half_inside
-            field = final[c, p : p + half_inside].reshape(half_inside * cn, cz)
-            acc = acc + gather(field, inner_ids(half_inside * cn, p * cn), 1)[0]
-        found_acc[c] = acc
-
-    loop(0, 3, gather_inside)
+    gather_inside(2)
     gather_inside(4)
     landed(second_vq)
     vq_two(0)
     vq_two(ce - 1)
-    loop(0, ce, lambda e: fix_vq(e, beside_second, final, 0, 0))
+    loop(0, ce, lambda e: fix_vq(e, beside_second, final, 0, 0), 4)
+    plane_iota = lax.broadcasted_iota(I32, (ce, slots), 0) * cn
+
+    def gather_edges(comps):
+        edge_ids = jnp.concatenate(
+            [inner_ids(cn, 0), inner_ids(cn, (ce - 1) * cn), plane_iota, plane_iota + cn - 1], axis=0
+        )
+        edge_fields = []
+        for c in comps:
+            edge_fields += [final[c, plane] for plane in (0, ce - 1)]
+            edge_fields += [final[c, :, row, :] for row in (0, cn - 1)]
+        return gather(jnp.concatenate(edge_fields, axis=0), edge_ids, len(comps))
+
+    edge_sums = gather_edges((0, 1, 2))
     landed(second_eddy)
     eddy_two(0)
     eddy_two(ce - 1)
-    loop(0, ce, lambda e: fix_eddy(e, beside_second, v1, final, 0, 0, False))
-
-    edge_fields = []
-    for c in (0, 1, 2, 4):
-        for plane in (0, ce - 1):
-            edge_fields.append(final[c, plane])
-        for row in (0, cn - 1):
-            edge_fields.append(final[c, :, row, :])
-    plane_iota = lax.broadcasted_iota(I32, (ce, slots), 0) * cn
-    edge_ids = jnp.concatenate(
-        [inner_ids(cn, 0), inner_ids(cn, (ce - 1) * cn), plane_iota, plane_iota + cn - 1], axis=0
-    )
-    edge_sums = gather(jnp.concatenate(edge_fields, axis=0), edge_ids, 4)
+    loop(0, ce, lambda e: fix_eddy(e, beside_second, v1, final, 0, 0, False), 4)
+
+    edge_sums += gather_edges((4,))
     values = [
         jnp.sum(found_acc[c] + edge, axis=0, keepdims=True) * factor for c, edge in zip((0, 1, 2, 4), edge_sums)
     ]
-    terms = jnp.concatenate(values + [jnp.zeros((4, slots), F32)], axis=0)
+    terms = jnp.concatenate(values + values, axis=0)
     both = jnp.concatenate(split(terms), axis=0)
-    spread = blocks[...] * jnp.concatenate([both] * n_north, axis=0)
+    spread = blocks[...] * jnp.concatenate([both] * n_plane, axis=0)
     contract = (((1,), (1,)), ((), ()))
     summed = lax.dot_general(spread, places[...], contract, preferred_element_type=F32)
-    summed = jnp.sum(summed.reshape(n_north, 2, 8, SECT * PITCH), axis=1)
-    parts[...] = summed.reshape(n_plane, 2, 8, SECT * PITCH)
+    parts[...] = jnp.sum(summed.reshape(n_plane, 2, 8, SECT * PITCH), axis=1)
 
     part_copies, total_copies = [], []
     for k in range(1, n_plane):
@@ -462,12 +483,18 @@
     for copy in part_copies:
         copy.start()
     gathered[in_plane] = parts[in_plane]
+    for group in (first_vq, first_base, first_eddy, second_vq, second_eddy):
+        left(group)
     for copy in part_copies:
         copy.wait_recv()
-    middle[...] = jnp.sum(gathered[...], axis=0)
+    in_middle = jnp.sum(gathered[...], axis=0)
+    middle[0] = in_middle[0:4]
+    middle[1] = in_middle[4:8]
     for copy in total_copies:
         copy.start()
     totals[in_line] = middle[low_z]
+    for copy in part_copies:
+        copy.wait_send()
     for copy in total_copies:
         copy.wait_recv()
     whole = jnp.sum(totals[...], axis=0)
@@ -476,10 +503,8 @@
         for c in range(4):
             grad[c, s : s + 1, :] = cut[c : c + 1]
 
-    for copy in part_copies + total_copies:
+    for copy in total_copies:
         copy.wait_send()
-    for group in (first_vq, first_base, first_eddy, second_vq, second_eddy):
-        left(group)
 
 
 def store(fields, sums, fields_out, sums_out, sem):
@@ -516,17 +541,17 @@
                 pltpu.VMEM((2 * cz, slots), BF16),
                 pltpu.VMEM((5, 8, slots), F32),
                 pltpu.VMEM((SECT * PITCH, slots), BF16),
-                pltpu.VMEM((n_north * 16, slots), BF16),
+                pltpu.VMEM((n_plane * 16, slots), BF16),
                 pltpu.VMEM((8, ce, 16, cz), F32),
                 pltpu.VMEM((5, ce, 16, cz), F32),
                 pltpu.VMEM((1, 1, slots), I32),
                 pltpu.VMEM((1, 1, slots), I32),
                 pltpu.VMEM((1, 1, slots), I32),
                 pltpu.VMEM((1, 1, slots), F32),
-                pltpu.VMEM((n_plane, 2, 8, SECT * PITCH), F32),
-                pltpu.VMEM((n_plane, 2, 8, SECT * PITCH), F32),
-                pltpu.VMEM((2, 8, SECT * PITCH), F32),
-                pltpu.VMEM((n_line, 8, SECT * PITCH), F32),
+                pltpu.VMEM((n_plane, 8, SECT * PITCH), F32),
+                pltpu.VMEM((n_plane, 8, SECT * PITCH), F32),
+                pltpu.VMEM((2, 4, SECT * PITCH), F32),
+                pltpu.VMEM((n_line, 4, SECT * PITCH), F32),
                 pltpu.SemaphoreType.DMA((9,)),
                 pltpu.SemaphoreType.DMA((2, 3, 4)),
                 pltpu.SemaphoreType.DMA((2, 3, 4)),

time: 43.2 us -> 42.3 us (0.979)
  Pallas kernels: 41.9 us -> 40.9 us
    pallas_call x1, Pallas kernels: 40.3 us -> 39.4 us  [shards(): pl.pallas_call(functools.partial(kernel, n_east, n_north), out_shape=(plt...]
where the time goes in v5:
time: 42.3 us; the launch traced here: 42.2 us
  Pallas kernels  40.9 us (97%)
  between operations  1.29 us (3%)
    pallas_call x1, Pallas kernels, shards(): pl.pallas_call(functools.partial(kernel, n_east, n_north), out_shape=(plt...  39.4 us
    pallas_call x1, Pallas kernels, shards(): pl.pallas_call(store, out_shape=tuple((jax.ShapeDtypeStruct(x.shape, x.dt...  1.54 us

profile of v5, /device:TPU:1, one launch (start us, length us, event | category | flops | bytes accessed | tf_op | source)
XLA Modules:
  0.0 42.2 jit_solution(5674202434053826949)
XLA Ops:
  1.3 39.4 %shard_map.104 = (f32[5,16,32,256]{3,2,1,0:T(8,128)S(1)}, f32[4,8,12]{2,1,0:T(8,128)S(1)}) custom-call(f32[5,16,32,256]{3,2,1,0:T(8,128)} %start.1, f32[5,16,32,256]{3,2,1,0:T(8,128)} %source.1, f32[3,16,32,256]{3,2,1,0:T(8,128)} %base.1, f32[16,32,256]{2,1,0:T(8,128)} %eddy.1, s32[1,1]{1,0:T(1,128)S(6)} %copy.11.count, s32[1,1,1024]{2,1,0:T(1,128)} %cell_in.1, ...), custom_call_target="tpu_custom_call" | custom-call | tf_op jit(solution)/shard_map/pallas_call | solution.py:527
  40.6 1.5 %shard_map.105 = (f32[5,16,32,256]{3,2,1,0:T(8,128)}, f32[4,8,12]{2,1,0:T(8,128)}) custom-call(f32[5,16,32,256]{3,2,1,0:T(8,128)S(1)} %get-tuple-element.4.fields, f32[4,8,12]{2,1,0:T(8,128)S(1)} %get-tuple-element.5.sums), custom_call_target="tpu_custom_call" | custom-call | tf_op jit(solution)/shard_map/pallas_call | solution.py:570
